TPU v7x, 256 devices: a whole 4x4x8 slice. The times are simulated.
256 devices in a mesh: tm: 32 (over x, y, core), space: 8 (over z).
Axes of the slice: x: 4, y: 4, z: 8, core: 2. Of those that a mesh axis runs over, the one named last changes fastest.
Arguments:
- sep_block: float32 [32, 1536, 1536], P('tm', 'space'), may hold values from -1 to 10, as said below
- own_couple: bfloat16 [32, 1536, 1536], P('tm', 'space'), may hold values from -0.1875 to 0.1875
- prev_couple: bfloat16 [32, 1536, 1536], P('tm', 'space'), may hold values from -0.1875 to 0.1875
- inner_diag: float32 [32, 1536], P('tm'), may hold values from 0.5 to 4
Outputs:
- reduced_blocks: float32 [32, 1536, 1536], P('tm', 'space')
- left_links: bfloat16 [32, 1536, 1536], P('tm', 'space')
Inputs may be any that keep to these rules, and one draw needn't show every extreme that they name: sep_block is symmetric in its last two dimensions; its diagonal entries lie between 3.5 and 10.
All inputs are finite; a program needn't handle non-finite values.
Results may differ from a plain program's by a relative error of at most 0.0083.
Values may be sent and summed in bfloat16 or wider, within the bound.
A program may use at most 64 MiB of HBM per device.

v0:
```python
import jax
import jax.numpy as jnp
from jax import lax
from jax.sharding import PartitionSpec as P


def passed_along(block, axis, distance):
    devices = range(lax.axis_size(axis))
    route = [(i - distance, i) for i in devices if i - distance in devices]
    return lax.ppermute(block, axis, route)


def scaled_by(matrix, factors):
    return (matrix.astype(jnp.float32) * factors.astype(jnp.float32)[None, :]).astype(jnp.bfloat16)


def outer_form(left_side, right_side):
    return jnp.einsum("ik,jk->ij", left_side, right_side, preferred_element_type=jnp.float32)


def reduce_level(schur, link, distance, partition, row_start):
    row_count = schur.shape[0]
    diag_block = lax.dynamic_slice_in_dim(schur, row_start, row_count, 1)
    scale_local = (1.0 / jnp.maximum(jnp.diagonal(diag_block), 1.0)).astype(jnp.bfloat16)
    scale_full = lax.all_gather(scale_local, "space", axis=0, tiled=True)
    own_full = lax.all_gather(link, "space", axis=0, tiled=True)
    next_full, next_scale = passed_along((own_full, scale_full), "tm", -distance)
    flipped = lax.dynamic_slice_in_dim(next_full, row_start, row_count, 1).T
    flipped_scaled = scaled_by(flipped, scale_full)
    right_form = jnp.dot(flipped_scaled, next_full, preferred_element_type=jnp.float32)
    own_scaled = scaled_by(link, scale_full)
    fill_link = (-jnp.dot(own_scaled, next_full, preferred_element_type=jnp.float32)).astype(
        jnp.bfloat16
    )
    right_recv, fill_recv = (
        passed_along(right_form.astype(jnp.bfloat16), "tm", distance).astype(right_form.dtype),
        passed_along(fill_link.astype(jnp.float32).astype(jnp.bfloat16), "tm", distance).astype(
            jnp.float32
        ),
    )
    next_local = lax.dynamic_slice_in_dim(next_full, row_start, row_count, 0)
    next_scaled = scaled_by(next_local, next_scale)
    left_form = outer_form(next_scaled, next_full)
    new_schur = schur - left_form - right_recv
    receiver = partition % (2 * distance) == 2 * distance - 1
    return (
        jnp.where(receiver, new_schur, schur),
        jnp.where(receiver, fill_recv.astype(jnp.bfloat16), link),
    )


def on_device(sep_block, own_couple, prev_couple, inner_diag):
    separator = sep_block[0]
    own_rows = own_couple[0]
    prev_rows = prev_couple[0]
    reciprocal = 1.0 / inner_diag[0]
    row_count = separator.shape[0]
    row_start = lax.axis_index("space") * row_count
    partition = lax.axis_index("tm")
    own_scaled = scaled_by(own_rows, reciprocal)
    prev_scaled = scaled_by(prev_rows, reciprocal)
    couple_pair = jnp.stack([own_rows, prev_rows])
    piece_rows = lax.all_gather(couple_pair, "space", axis=1, tiled=True)
    local_forms = jnp.stack(
        [
            outer_form(own_scaled, piece_rows[0]),
            outer_form(prev_scaled, piece_rows[1]),
            outer_form(prev_scaled, piece_rows[0]),
        ]
    )
    incoming = passed_along(local_forms[1], "tm", -1)
    schur = separator - local_forms[0] - incoming
    link = (-local_forms[2]).astype(jnp.bfloat16)
    link = jnp.where(partition == 0, jnp.zeros_like(link), link)
    for distance in (1, 2):
        schur, link = reduce_level(schur, link, distance, partition, row_start)
    return (schur[None], link[None])


def solution(mesh):
    placed = (P("tm", "space", None), P("tm", "space", None), P("tm", "space", None), P("tm", None))
    return jax.shard_map(
        on_device,
        mesh=mesh,
        in_specs=placed,
        out_specs=(P("tm", "space", None), P("tm", "space", None)),
        check_vma=False,
    )
```

profile of v0, /device:TPU:11, one launch (start us, length us, event | category | flops | bytes accessed | tf_op | source)
XLA Modules:
  0.0 513.7 jit_solution(10280945665940516997)
XLA Ops:
  10.3 106.9 %all-gather.4.cloned.1.call-done = bf16[2,1536,1536]{2,1,0:T(8,128)(2,1)} async-done(((bf16[2,192,1536]{2,1,0:T(8,128)(2,1)}), bf16[2,1536,1536]{2,1,0:T(8,128)(2,1)}) %all-gather.4.cloned.1.call-update) | async-done | bytes 9437200 | tf_op jit(solution)/shard_map/all_gather | solution.py:63
  117.2 4.8 fusion.14
  122.2 58.4 %all-gather.6.cloned.1.call-done = bf16[1536,1536]{1,0:T(8,128)(2,1)} async-done(((bf16[192,1536]{1,0:T(8,128)(2,1)}), bf16[1536,1536]{1,0:T(8,128)(2,1)}) %all-gather.6.cloned.1.call-update) | async-done | bytes 4718608 | tf_op jit(solution)/shard_map/all_gather | solution.py:26
  180.6 2.6 collective-permute-start.1
  183.2 5.0 fusion
  191.3 57.7 %collective-permute-done = f32[192,1536]{1,0:T(8,128)} collective-permute-done((f32[192,1536]{1,0:T(8,128)}, f32[192,1536]{1,0:T(8,128)}, u32[]{:S(2)}, u32[]{:S(2)}) %collective-permute-start) | collective-permute-done | bytes 1179680 | tf_op jit(solution)/shard_map/ppermute | solution.py:10
  249.0 4.4 fusion.4
  255.8 11.7 %all-reduce = bf16[1536]{0:T(1024)(128)(2,1)S(1)} all-reduce(bf16[1536]{0:T(1024)(128)(2,1)S(1)} %dynamic-update-slice), channel_id=1, replica_groups=mesh['tm'=32,'space'=8] {'space'}, use_global_device_ids=true, to_apply=%add | all-reduce | flops 1536 | bytes 6144
  267.6 3.4 fusion.12
  271.0 5.5 %collective-permute-start.4 = (bf16[192,1536]{1,0:T(8,128)(2,1)S(1)}, bf16[192,1536]{1,0:T(8,128)(2,1)S(1)}, u32[]{:S(2)}, u32[]{:S(2)}) collective-permute-start(bf16[192,1536]{1,0:T(8,128)(2,1)S(1)} %fusion.12), channel_id=1, source_target_pairs={{0,8},{8,16},{16,24},{24,32},{32,40},{40,48},{48,56},{56,64},{64,7... | collective-permute-start | bytes 1769480 | tf_op jit(solution)/shard_map/ppermute | solution.py:10
  276.5 6.8 %collective-permute-done.4 = bf16[192,1536]{1,0:T(8,128)(2,1)S(1)} collective-permute-done((bf16[192,1536]{1,0:T(8,128)(2,1)S(1)}, bf16[192,1536]{1,0:T(8,128)(2,1)S(1)}, u32[]{:S(2)}, u32[]{:S(2)}) %collective-permute-start.4) | collective-permute-done | bytes 589856 | tf_op jit(solution)/shard_map/ppermute | solution.py:10
  284.2 62.3 %all-gather.8.cloned.1.call-done = bf16[1536,1536]{1,0:T(8,128)(2,1)} async-done(((bf16[192,1536]{1,0:T(8,128)(2,1)}), bf16[1536,1536]{1,0:T(8,128)(2,1)}) %all-gather.8.cloned.1.call-update) | async-done | bytes 4718608 | tf_op jit(solution)/shard_map/all_gather | solution.py:26
  348.7 4.0 convolution_convert_fusion.1
  352.6 4.0 collective-permute-start.3
  358.5 94.0 %collective-permute-done.2 = bf16[1536]{0:T(1024)(128)(2,1)S(1)} collective-permute-done((bf16[1536]{0:T(1024)(128)(2,1)S(1)}, bf16[1536]{0:T(1024)(128)(2,1)S(1)}, u32[]{:S(2)}, u32[]{:S(2)}) %collective-permute-start.2) | collective-permute-done | bytes 3104 | tf_op jit(solution)/shard_map/ppermute | solution.py:10
  452.5 4.2 fusion.9
  459.1 11.8 %all-reduce.1 = bf16[1536]{0:T(1024)(128)(2,1)S(1)} all-reduce(bf16[1536]{0:T(1024)(128)(2,1)S(1)} %dynamic-update-slice.1), channel_id=1, replica_groups=mesh['tm'=32,'space'=8] {'space'}, use_global_device_ids=true, to_apply=%add.1 | all-reduce | flops 1536 | bytes 6144
  471.0 4.3 fusion.13
  475.2 3.1 collective-permute-start.8
  478.3 3.9 convolution_convert_fusion
  482.3 4.8 collective-permute-start.7
  489.1 2.7 collective-permute-done.6
  492.7 9.3 %collective-permute-done.7 = bf16[192,1536]{1,0:T(8,128)(2,1)S(1)} collective-permute-done((bf16[192,1536]{1,0:T(8,128)(2,1)S(1)}, bf16[192,1536]{1,0:T(8,128)(2,1)S(1)}, u32[]{:S(2)}, u32[]{:S(2)}) %collective-permute-start.7) | collective-permute-done | bytes 589856 | tf_op jit(solution)/shard_map/ppermute | solution.py:10
  501.9 5.2 %fusion.7 = f32[1,192,1536]{2,1,0:T(8,128)} fusion(f32[192,1536]{1,0:T(8,128)S(1)} %fusion.9, bf16[1536,1536]{1,0:T(8,128)(2,1)} %collective-permute-done.5, bf16[192,1536]{1,0:T(8,128)(2,1)S(1)} %collective-permute-done.7, f32[1536]{0:T(1024)S(1)} %convert_element_type.132, s32[]{:T(128)S(6)} %select_n.61, pred[]{:T(512)S(6)} %eq.12), kind=kOutput, calls=%fused_computation.14 | convolution fusion | flops 908034048 | bytes 8263685 | tf_op jit(solution)/shard_map/ik,jk->ij/dot_general | solution.py:18
  (48 shorter events, 18.1 us)
Async XLA Ops:
  7.2 110.0 %all-gather.4.cloned.1.call-start = ((), (), s32[]{:S(2)}) async-start(), calls=%async_computation | async-start | bytes 10616832 | tf_op jit(solution)/shard_map/all_gather | solution.py:63
  9.6 0.7 copy-start.5
  9.6 107.6 %copy-start.4 = (bf16[1,192,1536]{2,1,0:T(8,128)(2,1)S(1)}, bf16[1,192,1536]{2,1,0:T(8,128)(2,1)}, u32[]{:S(2)}) copy-start(bf16[1,192,1536]{2,1,0:T(8,128)(2,1)} %param.6) | copy-start | bytes 1769476
  9.6 171.0 %all-gather.6.cloned.1.call-start = ((), (), s32[]{:S(2)}) async-start(), calls=%async_computation.1 | async-start | bytes 5308416 | tf_op jit(solution)/shard_map/all_gather | solution.py:26
  122.1 68.1 %copy-start.6 = (u32[256]{0:T(256)S(1)}, u32[256]{0:T(256)}, u32[]{:S(2)}) copy-start(u32[256]{0:T(256)} %constant.83) | copy-start | bytes 3076
  122.1 126.9 %copy-start.1 = (bf16[1,192,1536]{2,1,0:T(8,128)(2,1)S(1)}, bf16[1,192,1536]{2,1,0:T(8,128)(2,1)}, u32[]{:S(2)}) copy-start(bf16[1,192,1536]{2,1,0:T(8,128)(2,1)} %param.5) | copy-start | bytes 1769476
  122.1 126.9 %copy-start.3 = (f32[1,192,1536]{2,1,0:T(8,128)S(1)}, f32[1,192,1536]{2,1,0:T(8,128)}, u32[]{:S(2)}) copy-start(f32[1,192,1536]{2,1,0:T(8,128)} %param.4) | copy-start | bytes 3538948
  122.1 224.4 %all-gather.8.cloned.1.call-start = ((), (), s32[]{:S(2)}) async-start(), calls=%async_computation.2 | async-start | bytes 5308416 | tf_op jit(solution)/shard_map/all_gather | solution.py:26
  180.6 87.0 %collective-permute-start.1 = (bf16[1536,1536]{1,0:T(8,128)(2,1)}, bf16[1536,1536]{1,0:T(8,128)(2,1)}, u32[]{:S(2)}, u32[]{:S(2)}) collective-permute-start(bf16[1536,1536]{1,0:T(8,128)(2,1)} %all-gather.6.cloned.1.call-done), channel_id=1, source_target_pairs={{8,0},{16,8},{24,16},{32,24},{40,32},{48,40},{56,48},{64,56},{72,6... | collective-permute-start | bytes 14155784 | tf_op jit(solution)/shard_map/ppermute | solution.py:10
  188.2 60.8 %collective-permute-start = (f32[192,1536]{1,0:T(8,128)}, f32[192,1536]{1,0:T(8,128)}, u32[]{:S(2)}, u32[]{:S(2)}) collective-permute-start(f32[192,1536]{1,0:T(8,128)} %fusion), channel_id=1, source_target_pairs={{8,0},{16,8},{24,16},{32,24},{40,32},{48,40},{56,48},{64,56},{72,6... | collective-permute-start | bytes 3538952 | tf_op jit(solution)/shard_map/ppermute | solution.py:10
  253.5 14.1 %copy-start.2 = (bf16[192,1536]{1,0:T(8,128)(2,1)S(1)}, bf16[192,1536]{1,0:T(8,128)(2,1)}, u32[]{:S(2)}) copy-start(bf16[192,1536]{1,0:T(8,128)(2,1)} %fusion.14) | copy-start | bytes 1769476
  271.0 12.3 %collective-permute-start.4 = (bf16[192,1536]{1,0:T(8,128)(2,1)S(1)}, bf16[192,1536]{1,0:T(8,128)(2,1)S(1)}, u32[]{:S(2)}, u32[]{:S(2)}) collective-permute-start(bf16[192,1536]{1,0:T(8,128)(2,1)S(1)} %fusion.12), channel_id=1, source_target_pairs={{0,8},{8,16},{16,24},{24,32},{32,40},{40,48},{48,56},{56,64},{64,7... | collective-permute-start | bytes 1769480 | tf_op jit(solution)/shard_map/ppermute | solution.py:10
  346.5 124.4 %collective-permute-start.5 = (bf16[1536,1536]{1,0:T(8,128)(2,1)}, bf16[1536,1536]{1,0:T(8,128)(2,1)}, u32[]{:S(2)}, u32[]{:S(2)}) collective-permute-start(bf16[1536,1536]{1,0:T(8,128)(2,1)} %all-gather.8.cloned.1.call-done), channel_id=1, source_target_pairs={{16,0},{24,8},{32,16},{40,24},{48,32},{56,40},{64,48},{72,56},{80,... | collective-permute-start | bytes 14155784 | tf_op jit(solution)/shard_map/ppermute | solution.py:10
  352.6 99.9 %collective-permute-start.3 = (bf16[192,1536]{1,0:T(8,128)(2,1)S(1)}, bf16[192,1536]{1,0:T(8,128)(2,1)S(1)}, u32[]{:S(2)}, u32[]{:S(2)}) collective-permute-start(bf16[192,1536]{1,0:T(8,128)(2,1)S(1)} %convolution_convert_fusion.1), channel_id=1, source_target_pairs={{0,8},{8,16},{16,24},{24,32},{32,40},{40,48},{48,56},{56,64},{64,7... | collective-permute-start | bytes 1769480 | tf_op jit(solution)/shard_map/ppermute | solution.py:10
  356.6 95.9 %collective-permute-start.2 = (bf16[1536]{0:T(1024)(128)(2,1)S(1)}, bf16[1536]{0:T(1024)(128)(2,1)S(1)}, u32[]{:S(2)}, u32[]{:S(2)}) collective-permute-start(bf16[1536]{0:T(1024)(128)(2,1)S(1)} %all-reduce), channel_id=1, source_target_pairs={{8,0},{16,8},{24,16},{32,24},{40,32},{48,40},{56,48},{64,56},{72,6... | collective-permute-start | bytes 9224 | tf_op jit(solution)/shard_map/ppermute | solution.py:10
  456.8 14.2 %copy-start = (bf16[192,1536]{1,0:T(8,128)(2,1)S(1)}, bf16[192,1536]{1,0:T(8,128)(2,1)}, u32[]{:S(2)}) copy-start(bf16[192,1536]{1,0:T(8,128)(2,1)} %broadcast_select_fusion) | copy-start | bytes 1769476
  475.2 16.6 %collective-permute-start.8 = (bf16[192,1536]{1,0:T(8,128)(2,1)}, bf16[192,1536]{1,0:T(8,128)(2,1)S(1)}, u32[]{:S(2)}, u32[]{:S(2)}) collective-permute-start(bf16[192,1536]{1,0:T(8,128)(2,1)} %fusion.13), channel_id=1, source_target_pairs={{0,16},{8,24},{16,32},{24,40},{32,48},{40,56},{48,64},{56,72},{64,... | collective-permute-start | bytes 1769480 | tf_op jit(solution)/shard_map/ppermute | solution.py:10
  482.3 19.6 %collective-permute-start.7 = (bf16[192,1536]{1,0:T(8,128)(2,1)S(1)}, bf16[192,1536]{1,0:T(8,128)(2,1)S(1)}, u32[]{:S(2)}, u32[]{:S(2)}) collective-permute-start(bf16[192,1536]{1,0:T(8,128)(2,1)S(1)} %convolution_convert_fusion), channel_id=1, source_target_pairs={{0,16},{8,24},{16,32},{24,40},{32,48},{40,56},{48,64},{56,72},{64,... | collective-permute-start | bytes 1769480 | tf_op jit(solution)/shard_map/ppermute | solution.py:10
  487.1 4.6 collective-permute-start.6
Sparse Core Ops, SparseCore 0:
  10.4 106.7 all-gather.3
  122.2 58.3 all-gather.5
  284.3 62.1 all-gather.7
where the time goes:
time: 521 us; the launch traced here: 514 us
  waiting for transfers between devices  398 us (76%)
  matrix products  39.4 us (8%)
  starting transfers between devices  28 us (5%)
  blocking collectives  23.6 us (5%)
  between operations  14.6 us (3%)
  local copies, waits for them, and re-layouts  5.8 us (1%)
    ppermute x9, waiting for transfers between devices, passed_along(): return lax.ppermute(block, axis, route)  170 us
    all_gather x2, waiting for transfers between devices, reduce_level(): own_full = lax.all_gather(link, 'space', axis=0, tiled=True)  121 us
    all_gather x1, waiting for transfers between devices, on_device(): piece_rows = lax.all_gather(couple_pair, 'space', axis=1, tiled=True)  107 us
    ppermute x9, starting transfers between devices, passed_along(): return lax.ppermute(block, axis, route)  27.9 us
    dot_general x5, matrix products, outer_form(): jnp.einsum('ik,jk->ij', left_side, right_side, preferred_element_type=jnp...  23.8 us
    unnamed x2, blocking collectives  23.6 us
  transfers between devices with their start and end apart: 12, of which 8 were waited for; matrix products, arithmetic and copies ran while one was open for 5% of the time, Pallas kernels for 0%

commit v1 on v0

v1 whole, which is shorter than its diff:
```python
import functools

import jax
import jax.numpy as jnp
from jax import lax
from jax.experimental import pallas as pl
from jax.experimental.pallas import tpu as pltpu
from jax.sharding import PartitionSpec as P

MESH = pl.DeviceIdType.MESH
OWN, PREV = 0, 1


def kernel(
    ring, parts, sep_hbm, own_hbm, prev_hbm, diag_ref, schur_ref, link_ref,
    sep, pair, scaled, links, links_scaled, fills, fills_scaled, sibling, handed, update,
    update_in, far, far_in, last, last_in, final, final_in,
    edge, edge_in, diags, edge2, edge2_in, diags2,
    load_sem, a_send, a_recv, w_send, w_recv, f_send, f_recv,
    d_send, d_recv, d2_send, d2_recv, e_send, e_recv, m_send, m_recv,
):
    rows, width = sep.shape
    tile = 512
    chunk = 16
    z = lax.axis_index("space")
    t = lax.axis_index("tm")
    odd = lax.rem(t, 2)
    role = lax.rem(t, 4)
    is_odd = odd == 1
    inner = jnp.logical_or(role == 1, role == 2)
    sib = t + 1 - 2 * odd
    across = lax.rem(t + 2 * odd - 1 + parts, parts)
    before = lax.rem(t + parts - 1, parts)
    before2 = lax.rem(t + parts - 2, parts)
    after = lax.rem(t + 1, parts)
    after2 = lax.rem(t + 2, parts)

    barrier = pltpu.get_barrier_semaphore()
    for k in range(1, ring):
        pl.semaphore_signal(
            barrier, inc=1, device_id={"space": lax.rem(z + k, ring)}, device_id_type=MESH
        )
    for peer in (before, before2, after, after2):
        pl.semaphore_signal(barrier, inc=1, device_id={"tm": peer}, device_id_type=MESH)

    def mine(step):
        return pl.ds(pl.multiple_of(step * rows, rows), rows)

    loads = [
        pltpu.make_async_copy(own_hbm, pair.at[OWN, mine(z)], load_sem.at[0]),
        pltpu.make_async_copy(prev_hbm, pair.at[PREV, mine(z)], load_sem.at[1]),
        pltpu.make_async_copy(sep_hbm, sep, load_sem.at[2]),
    ]
    for load in loads:
        load.start()
    for load in loads:
        load.wait()
    pl.semaphore_wait(barrier, ring + 3)

    def hop(buf, offset, count, way, step, send_sem, recv_sem):
        slot = lax.rem(z - way * (step - 1) + 2 * ring, ring)
        piece = buf.at[pl.ds(pl.multiple_of(slot * rows + offset, chunk), count)]
        return pltpu.make_async_remote_copy(
            src_ref=piece, dst_ref=piece, send_sem=send_sem, recv_sem=recv_sem,
            device_id={"space": lax.rem(z + way + ring, ring)}, device_id_type=MESH,
        )

    class Ring:
        def __init__(self, streams, send_sem, recv_sem):
            self.streams = streams
            self.sems = send_sem, recv_sem

        def at(self, s, step):
            buf, offset, count, way, _ = self.streams[s]
            at = s * (ring // 2) + step - 1
            return hop(buf, offset, count, way, step, self.sems[0].at[at], self.sems[1].at[at])

        def start(self):
            for s in range(len(self.streams)):
                self.at(s, 1).start()

        def run(self):
            for step in range(1, ring // 2 + 1):
                for s, stream in enumerate(self.streams):
                    if step <= stream[4]:
                        self.at(s, step).wait_recv()
                        if step < stream[4]:
                            self.at(s, step + 1).start()

        def drain(self):
            for s, stream in enumerate(self.streams):
                for step in range(1, stream[4] + 1):
                    self.at(s, step).wait_send()

    far_way, near_way = ring // 2, ring // 2 - 1

    def both_ways(buf):
        half = rows // 2
        return [
            (buf, 0, half, 1, far_way),
            (buf, 0, half, -1, near_way),
            (buf, half, half, -1, far_way),
            (buf, half, half, 1, near_way),
        ]

    ring_a = Ring(
        [
            (pair.at[OWN], 0, rows, 1, far_way),
            (pair.at[PREV], 0, rows, -1, far_way),
            (pair.at[OWN], 0, rows, -1, near_way),
            (pair.at[PREV], 0, rows, 1, near_way),
        ],
        a_send, a_recv,
    )
    ring_w = Ring(both_ways(links), w_send, w_recv)
    ring_f = Ring(both_ways(fills), f_send, f_recv)
    ring_a.start()

    def to_part(src, dst, k, peer):
        return pltpu.make_async_remote_copy(
            src_ref=src, dst_ref=dst, send_sem=m_send.at[k], recv_sem=m_recv.at[k],
            device_id={"tm": peer}, device_id_type=MESH,
        )

    def diag_part(out, sep_factor, terms):
        out[...] = jnp.zeros_like(out)

        @pl.loop(0, rows // chunk)
        def _(i):
            at = pl.multiple_of(i * chunk, chunk)
            total = jnp.zeros((chunk, 1), jnp.float32)
            for left, right in terms:
                total += jnp.sum(
                    left(at).astype(jnp.float32) * right(at).astype(jnp.float32),
                    axis=1, keepdims=True,
                )
            spot = lax.broadcasted_iota(jnp.int32, (chunk, width), 1) == (
                lax.broadcasted_iota(jnp.int32, (chunk, width), 0) + (z * rows + at)
            )
            values = sep[pl.ds(at, chunk), :] * sep_factor - total
            out[...] += jnp.sum(jnp.where(spot, values, 0.0), axis=0, keepdims=True)

    def spread(edge, edge_in, diags, peer, k, sems):
        copy = pltpu.make_async_remote_copy(
            src_ref=edge, dst_ref=edge_in, send_sem=e_send.at[k], recv_sem=e_recv.at[k],
            device_id={"tm": peer}, device_id_type=MESH,
        )
        copy.start()
        copy.wait()
        diags[z] = edge[...] + edge_in[...]
        for s in range(1, ring):
            spread_copy(diags, s, sems).start()

    def spread_copy(diags, s, sems):
        return pltpu.make_async_remote_copy(
            src_ref=diags.at[z], dst_ref=diags.at[z], send_sem=sems[0].at[s - 1],
            recv_sem=sems[1].at[s - 1],
            device_id={"space": lax.rem(z + s, ring)}, device_id_type=MESH,
        )

    def pivot_scale(diags, sems):
        for s in range(1, ring):
            spread_copy(diags, s, sems).wait_recv()
        values = diags[0]
        for s in range(1, ring):
            values += diags[s]
        return (1.0 / jnp.maximum(values, 1.0)).astype(jnp.bfloat16).astype(jnp.float32)

    def scale_rows(source, factors, out):
        @pl.loop(0, rows // chunk)
        def _(i):
            at = pl.multiple_of(i * chunk, chunk)
            out(at)[...] = (source(at)[...].astype(jnp.float32) * factors).astype(jnp.bfloat16)

    def product(left, right, take):
        @pl.loop(0, width // tile)
        def _(j):
            at = pl.multiple_of(j * tile, tile)
            take(
                pl.ds(at, tile),
                lax.dot_general(
                    left[...], right[pl.ds(at, tile), :], (((1,), (1,)), ((), ())),
                    preferred_element_type=jnp.float32,
                ),
            )

    reciprocal = 1.0 / diag_ref[...]
    for which in (OWN, PREV):
        scale_rows(
            lambda at: pair.at[which, pl.ds(pl.multiple_of(z * rows + at, chunk), chunk)],
            reciprocal,
            lambda at: scaled.at[which, pl.ds(at, chunk)],
        )

    def form_rows(which):
        return (
            lambda at: scaled[which, pl.ds(at, chunk), :],
            lambda at: pair[which, pl.ds(pl.multiple_of(z * rows + at, chunk), chunk), :],
        )

    first, second = 1 - odd, odd
    diag_part(edge, (1 - odd).astype(jnp.float32), [form_rows(second)])
    spread(edge, edge_in, diags, sib, 0, (d_send, d_recv))
    ring_a.run()

    sign = jnp.where(t == 0, 0.0, -1.0)
    my_links = links.at[mine(z)]
    my_fills = fills.at[mine(z)]

    def take_link(at, value):
        my_links[:, at] = (value * sign).astype(jnp.bfloat16)

    product(scaled.at[first], pair.at[second], take_link)
    ring_w.start()
    scale1 = pivot_scale(diags, (d_send, d_recv))
    scale_rows(
        lambda at: my_links.at[pl.ds(at, chunk)], scale1, lambda at: links_scaled.at[pl.ds(at, chunk)]
    )
    hand = to_part(links_scaled, sibling, 0, sib)

    @pl.when(jnp.logical_not(inner))
    def _():
        hand.start()

    @pl.when(inner)
    def _():
        diag_part(
            edge2, odd.astype(jnp.float32),
            [
                form_rows(first),
                (
                    lambda at: links_scaled[pl.ds(at, chunk), :],
                    lambda at: links[pl.ds(pl.multiple_of(z * rows + at, chunk), chunk), :],
                ),
            ],
        )
        spread(edge2, edge2_in, diags2, across, 1, (d2_send, d2_recv))

    def take_own(at, value):
        schur_ref[:, at] = sep[:, at] - value

    def take_prev(at, value):
        update[:, at] = value.astype(jnp.bfloat16)

    def take_prev_wide(at, value):
        sep[:, at] = value

    product(scaled.at[OWN], pair.at[OWN], take_own)
    send_update = to_part(update, update_in, 1, before)

    @pl.when(is_odd)
    def _():
        product(scaled.at[PREV], pair.at[PREV], take_prev)
        send_update.start()

    @pl.when(jnp.logical_not(is_odd))
    def _():
        product(scaled.at[PREV], pair.at[PREV], take_prev_wide)
        link_ref[...] = my_links[...]

    ring_w.run()
    hand_fill = to_part(fills_scaled, handed, 2, after)

    @pl.when(inner)
    def _():
        hand.wait_recv()

        def take_fill(at, value):
            my_fills[:, at] = (-value).astype(jnp.bfloat16)

        product(sibling, links, take_fill)
        ring_f.start()
        scale2 = pivot_scale(diags2, (d2_send, d2_recv))
        scale_rows(
            lambda at: my_fills.at[pl.ds(at, chunk)], scale2,
            lambda at: fills_scaled.at[pl.ds(at, chunk)],
        )

    @pl.when(role == 1)
    def _():
        hand_fill.start()
        link_ref[...] = my_fills[...]

    @pl.when(is_odd)
    def _():
        def take(at, value):
            schur_ref[:, at] -= value

        product(links_scaled, links, take)

    @pl.when(jnp.logical_not(is_odd))
    def _():
        def take(at, value):
            update[:, at] = (sep[:, at] + value).astype(jnp.bfloat16)

        product(links_scaled, links, take)
        send_update.start()

    @pl.when(inner)
    def _():
        ring_f.run()

    send_far = to_part(far, far_in, 3, before2)
    send_last = to_part(last, last_in, 4, after)
    send_final = to_part(final, final_in, 5, after)

    @pl.when(role == 1)
    def _():
        def take(at, value):
            far[:, at] = value.astype(jnp.bfloat16)

        product(fills_scaled, fills, take)
        send_far.start()

    @pl.when(role == 2)
    def _():
        def take(at, value):
            last[:, at] = value.astype(jnp.bfloat16)

        product(fills_scaled, fills, take)
        send_last.start()
        hand_fill.wait_recv()

        def take_final(at, value):
            final[:, at] = (-value).astype(jnp.bfloat16)

        product(handed, fills, take_final)
        send_final.start()

    send_update.wait_recv()

    @pl.when(t != parts - 1)
    def _():
        schur_ref[...] -= update_in[...].astype(jnp.float32)

    @pl.when(role == 3)
    def _():
        send_far.wait_recv()
        send_last.wait_recv()

        @pl.when(t != parts - 1)
        def _():
            schur_ref[...] -= far_in[...].astype(jnp.float32)

        schur_ref[...] -= last_in[...].astype(jnp.float32)
        send_final.wait_recv()
        link_ref[...] = final_in[...]

    ring_a.drain()
    ring_w.drain()
    send_update.wait_send()
    for s in range(1, ring):
        spread_copy(diags, s, (d_send, d_recv)).wait_send()

    @pl.when(inner)
    def _():
        ring_f.drain()
        for s in range(1, ring):
            spread_copy(diags2, s, (d2_send, d2_recv)).wait_send()

    @pl.when(jnp.logical_not(inner))
    def _():
        hand.wait_send()

    @pl.when(role == 1)
    def _():
        hand_fill.wait_send()
        send_far.wait_send()

    @pl.when(role == 2)
    def _():
        send_last.wait_send()
        send_final.wait_send()


def solution(mesh):
    ring, parts = mesh.shape["space"], mesh.shape["tm"]

    def on_device(sep_block, own_couple, prev_couple, inner_diag):
        rows, width = sep_block.shape[1:]

        def block(kind, *lead):
            return pltpu.VMEM((*lead, rows, width), kind)

        def full(*lead):
            return pltpu.VMEM((*lead, width, width), jnp.bfloat16)

        line = pltpu.VMEM((1, width), jnp.float32)
        lines = pltpu.VMEM((ring, 1, width), jnp.float32)
        half = jnp.bfloat16
        hops = pltpu.SemaphoreType.DMA((4 * (ring // 2),))
        peers = pltpu.SemaphoreType.DMA((ring - 1,))
        schur, link = pl.pallas_call(
            functools.partial(kernel, ring, parts),
            out_shape=(
                jax.ShapeDtypeStruct((rows, width), jnp.float32),
                jax.ShapeDtypeStruct((rows, width), half),
            ),
            in_specs=[pl.BlockSpec(memory_space=pl.ANY)] * 3
            + [pl.BlockSpec(memory_space=pltpu.VMEM)],
            out_specs=(pl.BlockSpec(memory_space=pltpu.VMEM),) * 2,
            scratch_shapes=[
                block(jnp.float32), full(2), block(half, 2), full(), block(half), full(), block(half),
                block(half), block(half), block(half), block(half), block(half), block(half),
                block(half), block(half), block(half), block(half),
                line, line, lines, line, line, lines,
                pltpu.SemaphoreType.DMA((3,)), hops, hops, hops, hops, hops, hops,
                peers, peers, peers, peers,
                pltpu.SemaphoreType.DMA((2,)), pltpu.SemaphoreType.DMA((2,)),
                pltpu.SemaphoreType.DMA((6,)), pltpu.SemaphoreType.DMA((6,)),
            ],
            compiler_params=pltpu.CompilerParams(
                collective_id=0, has_side_effects=True, vmem_limit_bytes=56 * 2**20
            ),
            cost_estimate=pl.CostEstimate(
                flops=7 * 2 * rows * width * width, bytes_accessed=10 * rows * width, transcendentals=0
            ),
        )(sep_block[0], own_couple[0], prev_couple[0], inner_diag)
        return schur[None], link[None]

    placed = (P("tm", "space", None), P("tm", "space", None), P("tm", "space", None), P("tm", None))
    return jax.shard_map(
        on_device,
        mesh=mesh,
        in_specs=placed,
        out_specs=(P("tm", "space", None), P("tm", "space", None)),
        check_vma=False,
    )
```

time: 521 us -> 192 us (0.37); the launches traced: 514 us -> 190 us
  waiting for transfers between devices: 398 us -> 0 us
  Pallas kernels: 0 us -> 187 us
  matrix products: 39.4 us -> 0 us
  starting transfers between devices: 28 us -> 0 us
  blocking collectives: 23.6 us -> 0 us
  between operations: 14.6 us -> 0.65 us
    all_gather x3 -> x0, waiting for transfers between devices: 228 us -> none  [the longest x2 121 us: reduce_level(): own_full = lax.all_gather(link, 'space', axis=0, tiled=True)]
    pallas_call x0 -> x1, Pallas kernels: none -> 187 us  [on_device(): pl.pallas_call(functools.partial(kernel, ring, parts), out_shape=(jax.Sha...]
    ppermute x9 -> x0, waiting for transfers between devices: 170 us -> none  [passed_along(): return lax.ppermute(block, axis, route)]
    dot_general x9 -> x0, matrix products: 39.4 us -> none  [the longest x5 23.8 us: outer_form(): jnp.einsum('ik,jk->ij', left_side, right_side, preferred_element_type=jnp...]
    ppermute x9 -> x0, starting transfers between devices: 27.9 us -> none  [passed_along(): return lax.ppermute(block, axis, route)]
    unnamed x2 -> x0, blocking collectives: 23.6 us -> none
  transfers between devices with their start and end apart: 12 -> 0, of which waited for: 8 -> 0; matrix products, arithmetic and copies ran while one was open for 5% -> 0% of each run, Pallas kernels for 0% -> 0%
where the time goes in v1:
time: 192 us; the launch traced here: 190 us
  Pallas kernels  187 us (97%)
  local copies, waits for them, and re-layouts  3.24 us (2%)
    pallas_call x1, Pallas kernels, on_device(): pl.pallas_call(functools.partial(kernel, ring, parts), out_shape=(jax.Sha...  187 us

profile of v1, /device:TPU:11, one launch (start us, length us, event | category | flops | bytes accessed | tf_op | source)
XLA Modules:
  0.0 190.4 jit_solution(14797155114419074)
XLA Ops:
  0.6 186.6 %shard_map.59 = (f32[192,1536]{1,0:T(8,128)}, bf16[192,1536]{1,0:T(8,128)(2,1)}) custom-call(f32[192,1536]{1,0:T(8,128)} %bitcast.7, bf16[192,1536]{1,0:T(8,128)(2,1)} %bitcast.8, bf16[192,1536]{1,0:T(8,128)(2,1)} %bitcast.9, f32[1,1536]{1,0:T(1,128)} %diag_ref.1), custom_call_target="tpu_custom_call" | custom-call | flops 6341787648 | bytes 2949120 | tf_op jit(solution)/shard_map/pallas_call | solution.py:393
  187.2 0.0 copy-start
  187.2 2.4 %copy.8 = f32[1,192,1536]{2,1,0:T(8,128)} copy(f32[1,192,1536]{2,1,0:T(8,128)} %bitcast.5) | data formatting | bytes 2359296
  189.6 0.0 copy-done
  189.6 0.8 copy.9
Async XLA Ops:
  187.2 2.4 %copy-start = (bf16[192,1536]{1,0:T(8,128)(2,1)S(1)}, bf16[192,1536]{1,0:T(8,128)(2,1)}, u32[]{:S(2)}) copy-start(bf16[192,1536]{1,0:T(8,128)(2,1)} %get-tuple-element.5) | copy-start | bytes 1769476

commit v2 on v1

v2 whole, which is shorter than its diff:
```python
import functools

import jax
import jax.numpy as jnp
from jax import lax
from jax.experimental import pallas as pl
from jax.experimental.pallas import tpu as pltpu
from jax.sharding import PartitionSpec as P

MESH = pl.DeviceIdType.MESH
OWN, PREV = 0, 1


def kernel(
    ring, parts, sep_hbm, own_hbm, prev_hbm, diag_ref, schur_ref, link_ref,
    sep, pair, scaled, links, links_scaled, sibling, fills, fills_scaled, handed,
    link_cells, form_cells, fill_cells, square_cells, update, update_in,
    far, far_in, last, last_in, final, final_in,
    link_out, form_out, fill_out, square_out,
    edge, edge_in, diags, edge2, edge2_in, diags2,
    load_sem, a_send, a_recv, w_send, w_recv, f_send, f_recv,
    d_send, d_recv, d2_send, d2_recv, e_send, e_recv, hand_send, hand_recv,
    r_send, r_recv, m_send, m_recv, t_send, t_recv,
):
    rows, width = sep.shape
    chunk = 16
    z = lax.axis_index("space")
    t = lax.axis_index("tm")
    odd = lax.rem(t, 2)
    role = lax.rem(t, 4)
    is_odd = odd == 1
    inner = jnp.logical_or(role == 1, role == 2)
    sib = t + 1 - 2 * odd
    across = lax.rem(t + 2 * odd - 1 + parts, parts)
    before = lax.rem(t + parts - 1, parts)
    before2 = lax.rem(t + parts - 2, parts)
    after = lax.rem(t + 1, parts)
    after2 = lax.rem(t + 2, parts)
    first, second = 1 - odd, odd

    barrier = pltpu.get_barrier_semaphore()
    for k in range(1, ring):
        pl.semaphore_signal(
            barrier, inc=1, device_id={"space": lax.rem(z + k, ring)}, device_id_type=MESH
        )
    for peer in (before, before2, after, after2):
        pl.semaphore_signal(barrier, inc=1, device_id={"tm": peer}, device_id_type=MESH)

    def near(d):
        return lax.rem(z + d + ring, ring)

    def row_slice(d):
        return pl.ds(pl.multiple_of(near(d) * rows, rows), rows)

    def cell_columns(j):
        return slice(j * rows, (j + 1) * rows)

    loads = [
        pltpu.make_async_copy(own_hbm, pair.at[OWN, row_slice(0)], load_sem.at[0]),
        pltpu.make_async_copy(prev_hbm, pair.at[PREV, row_slice(0)], load_sem.at[1]),
        pltpu.make_async_copy(sep_hbm, sep, load_sem.at[2]),
    ]
    for load in loads:
        load.start()
    for load in loads:
        load.wait()
    pl.semaphore_wait(barrier, ring + 3)

    def along(src, dst, way, send_sem, recv_sem):
        return pltpu.make_async_remote_copy(
            src_ref=src, dst_ref=dst, send_sem=send_sem, recv_sem=recv_sem,
            device_id={"space": near(way)}, device_id_type=MESH,
        )

    class Ring:
        def __init__(self, streams, send_sem, recv_sem):
            self.streams = streams
            self.sems = send_sem, recv_sem

        def at(self, s, step):
            buf, offset, count, way, _ = self.streams[s]
            at = s * (ring // 2) + step - 1
            slot = near(-way * (step - 1))
            piece = buf.at[pl.ds(pl.multiple_of(slot * rows + offset, chunk), count)]
            return along(piece, piece, way, self.sems[0].at[at], self.sems[1].at[at])

        def start(self):
            for s in range(len(self.streams)):
                self.at(s, 1).start()

        def arrive(self, step, which=None):
            for s, stream in enumerate(self.streams):
                if step <= stream[4] and (which is None or s in which):
                    self.at(s, step).wait_recv()
                    if step < stream[4]:
                        self.at(s, step + 1).start()

        def drain(self):
            for s, stream in enumerate(self.streams):
                for step in range(1, stream[4] + 1):
                    self.at(s, step).wait_send()

    half = rows // 2
    ring_a = Ring(
        [
            (pair.at[first], 0, rows, 1, 2),
            (pair.at[first], 0, rows, -1, 2),
            (pair.at[second], 0, rows, 1, 2),
            (pair.at[second], 0, rows, -1, 2),
        ],
        a_send, a_recv,
    )
    ring_w = Ring(
        [
            (links, 0, half, 1, 2),
            (links, 0, half, -1, 2),
            (links, half, half, 1, 2),
            (links, half, half, -1, 2),
        ],
        w_send, w_recv,
    )
    ring_f = Ring(
        [
            (fills, 0, half, 1, ring // 2),
            (fills, half, half, -1, ring // 2),
            (fills, 0, half, -1, ring // 2 - 1),
            (fills, half, half, 1, ring // 2 - 1),
        ],
        f_send, f_recv,
    )
    ring_a.start()

    def to_part(src, dst, peer, send_sem, recv_sem):
        return pltpu.make_async_remote_copy(
            src_ref=src, dst_ref=dst, send_sem=send_sem, recv_sem=recv_sem,
            device_id={"tm": peer}, device_id_type=MESH,
        )

    def diag_part(out, sep_factor, terms):
        out[...] = jnp.zeros_like(out)

        @pl.loop(0, rows // chunk)
        def _(i):
            at = pl.multiple_of(i * chunk, chunk)
            total = jnp.zeros((chunk, 1), jnp.float32)
            for left, right in terms:
                total += jnp.sum(
                    left(at).astype(jnp.float32) * right(at).astype(jnp.float32),
                    axis=1, keepdims=True,
                )
            spot = lax.broadcasted_iota(jnp.int32, (chunk, width), 1) == (
                lax.broadcasted_iota(jnp.int32, (chunk, width), 0) + (z * rows + at)
            )
            values = sep[pl.ds(at, chunk), :] * sep_factor - total
            out[...] += jnp.sum(jnp.where(spot, values, 0.0), axis=0, keepdims=True)

    def spread(edge, edge_in, diags, peer, k, sems):
        copy = to_part(edge, edge_in, peer, e_send.at[k], e_recv.at[k])
        copy.start()
        copy.wait()
        diags[z] = edge[...] + edge_in[...]
        for s in range(1, ring):
            spread_copy(diags, s, sems).start()

    def spread_copy(diags, s, sems):
        return along(diags.at[z], diags.at[z], s, sems[0].at[s - 1], sems[1].at[s - 1])

    def pivot_scale(diags, sems):
        for s in range(1, ring):
            spread_copy(diags, s, sems).wait_recv()
        values = diags[0]
        for s in range(1, ring):
            values += diags[s]
        return (1.0 / jnp.maximum(values, 1.0)).astype(jnp.bfloat16).astype(jnp.float32)

    def scale_rows(source, factors, out):
        @pl.loop(0, rows // chunk)
        def _(i):
            at = pl.ds(pl.multiple_of(i * chunk, chunk), chunk)
            out[at, :] = (source[at, :].astype(jnp.float32) * factors).astype(jnp.bfloat16)

    def dot(left, right):
        return lax.dot_general(
            left[...], right[...], (((1,), (1,)), ((), ())), preferred_element_type=jnp.float32
        )

    lanes = {0: slice(0, rows), 1: slice(rows, 2 * rows)}
    scaled_at = {0: 0, -1: 1, 1: 2, 2: 3}

    def put(cells, index, value, part=0):
        cells[index, :, lanes[part]] = value.astype(jnp.bfloat16)

    def returned(out, cells, k, group, long_way):
        way = (-1, 1, long_way)[k]
        col = (2, -2, -long_way)[k]
        at = 3 * group + k
        return along(out.at[k], cells.at[near(col)], way, r_send.at[at], r_recv.at[at])

    reciprocal = 1.0 / diag_ref[...]

    def scale_pair(which, d):
        scale_rows(pair.at[which, row_slice(d)], reciprocal, scaled.at[which, scaled_at[d]])

    def pair_rows(which, d):
        return pair.at[which, row_slice(d)]

    def link_rows(d):
        return links.at[row_slice(d)]

    scale_pair(OWN, 0)
    scale_pair(PREV, 0)

    def form_rows(which):
        mine = pair.at[which, row_slice(0)]
        return (
            lambda at: scaled[which, 0, pl.ds(at, chunk), :],
            lambda at: mine[pl.ds(at, chunk), :],
        )

    diag_part(edge, (1 - odd).astype(jnp.float32), [form_rows(second)])
    spread(edge, edge_in, diags, sib, 0, (d_send, d_recv))

    sign = jnp.where(t == 0, 0.0, -1.0)

    def link_cell(d):
        put(link_cells, near(d), dot(scaled.at[first, 0], pair_rows(second, d)) * sign)

    def form_cell(d):
        for which in (OWN, PREV):
            put(form_cells, near(d), dot(scaled.at[which, 0], pair_rows(which, d)), which)

    link_cell(0)
    form_cell(0)
    ring_a.arrive(1)
    for d in (-1, 1):
        scale_pair(OWN, d)
        scale_pair(PREV, d)
        link_cell(d)
        form_cell(d)
    ring_a.arrive(2, (0, 1))
    scale_pair(first, 2)
    ring_a.arrive(2, (2, 3))
    for k, (row, col) in enumerate(((-1, 2), (1, -2), (2, -2))):
        put(link_out, k, dot(scaled.at[first, scaled_at[row]], pair_rows(second, col)) * sign)
        returned(link_out, link_cells, k, 0, 2).start()
    link_cell(-2)
    link_cell(2)
    scale_pair(second, 2)
    for k, (row, col) in enumerate(((-1, 2), (1, -2))):
        for which in (OWN, PREV):
            put(form_out, k, dot(scaled.at[which, scaled_at[row]], pair_rows(which, col)), which)
        returned(form_out, form_cells, k, 1, -2).start()
    for which in (OWN, PREV):
        put(form_out, 2, dot(pair_rows(which, -2), scaled.at[which, scaled_at[2]]), which)
    returned(form_out, form_cells, 2, 1, -2).start()

    my_links = link_rows(0)
    my_fills = fills.at[row_slice(0)]
    for k in range(3):
        returned(link_out, link_cells, k, 0, 2).wait_recv()
    for j in range(ring):
        my_links[:, cell_columns(j)] = link_cells[j, :, lanes[0]]
    ring_w.start()

    scale1 = pivot_scale(diags, (d_send, d_recv))

    def hand(d):
        k = scaled_at[d]
        return to_part(links_scaled.at[k], sibling.at[k], sib, hand_send.at[k], hand_recv.at[k])

    def scale_link(d):
        scale_rows(link_rows(d), scale1, links_scaled.at[scaled_at[d]])

        @pl.when(jnp.logical_not(inner))
        def _():
            hand(d).start()

    def square_cell(d):
        put(square_cells, near(d), dot(links_scaled.at[0], link_rows(d)))

    def fill_cell(d):
        put(fill_cells, near(d), -dot(sibling.at[0], link_rows(d)))

    scale_link(0)

    @pl.when(inner)
    def _():
        mine = link_rows(0)
        diag_part(
            edge2, odd.astype(jnp.float32),
            [
                form_rows(first),
                (
                    lambda at: links_scaled[0, pl.ds(at, chunk), :],
                    lambda at: mine[pl.ds(at, chunk), :],
                ),
            ],
        )
        spread(edge2, edge2_in, diags2, across, 1, (d2_send, d2_recv))
        hand(0).wait_recv()
        fill_cell(0)

    square_cell(0)
    ring_w.arrive(1)
    for d in (-1, 1):
        scale_link(d)

    @pl.when(inner)
    def _():
        fill_cell(-1)
        fill_cell(1)

    for d in (-1, 1):
        square_cell(d)
    form_cell(-2)
    form_cell(2)

    @pl.when(jnp.logical_not(is_odd))
    def _():
        link_ref[...] = my_links[...]

    ring_w.arrive(2)
    scale_link(2)

    @pl.when(inner)
    def _():
        for d in (-1, 1, 2):
            hand(d).wait_recv()
        for k, (row, col) in enumerate(((-1, 2), (1, -2), (2, -2))):
            put(fill_out, k, -dot(sibling.at[scaled_at[row]], link_rows(col)))
            returned(fill_out, fill_cells, k, 2, 2).start()
        fill_cell(-2)
        fill_cell(2)

    for k, (row, col) in enumerate(((-1, 2), (1, -2))):
        put(square_out, k, dot(links_scaled.at[scaled_at[row]], link_rows(col)))
        returned(square_out, square_cells, k, 3, -2).start()
    put(square_out, 2, dot(link_rows(-2), links_scaled.at[scaled_at[2]]))
    returned(square_out, square_cells, 2, 3, -2).start()

    hand_fill = to_part(fills_scaled, handed, after, m_send.at[0], m_recv.at[0])

    @pl.when(inner)
    def _():
        for k in range(3):
            returned(fill_out, fill_cells, k, 2, 2).wait_recv()
        for j in range(ring):
            my_fills[:, cell_columns(j)] = fill_cells[j, :, lanes[0]]
        ring_f.start()
        scale_rows(my_fills, pivot_scale(diags2, (d2_send, d2_recv)), fills_scaled)

    @pl.when(role == 1)
    def _():
        hand_fill.start()
        link_ref[...] = my_fills[...]

    square_cell(-2)
    square_cell(2)
    for k in range(3):
        returned(form_out, form_cells, k, 1, -2).wait_recv()
        returned(square_out, square_cells, k, 3, -2).wait_recv()
    send_update = to_part(update, update_in, before, m_send.at[1], m_recv.at[1])

    @pl.when(is_odd)
    def _():
        for j in range(ring):
            at = cell_columns(j)
            taken = form_cells[j, :, lanes[OWN]].astype(jnp.float32)
            taken += square_cells[j, :, lanes[0]].astype(jnp.float32)
            schur_ref[:, at] = sep[:, at] - taken
            update[j, :, lanes[0]] = form_cells[j, :, lanes[PREV]]

    @pl.when(jnp.logical_not(is_odd))
    def _():
        for j in range(ring):
            at = cell_columns(j)
            schur_ref[:, at] = sep[:, at] - form_cells[j, :, lanes[OWN]].astype(jnp.float32)
            total = form_cells[j, :, lanes[PREV]].astype(jnp.float32)
            total += square_cells[j, :, lanes[0]].astype(jnp.float32)
            put(update, j, total)

    send_update.start()

    order = [0]
    for step in range(1, ring // 2):
        order += [-step, step]
    order.append(ring // 2)

    def handed_on(src, dst, peer, group, i):
        j = near(order[i])
        at = group * ring + i
        return to_part(src.at[j], dst.at[j], peer, t_send.at[at], t_recv.at[at])

    def last_cells(which):
        @pl.when(role == 1)
        def _():
            for i in which:
                put(far, near(order[i]), dot(fills_scaled, fills.at[row_slice(order[i])]))
                handed_on(far, far_in, before2, 0, i).start()

        @pl.when(role == 2)
        def _():
            for i in which:
                right = fills.at[row_slice(order[i])]
                put(last, near(order[i]), dot(fills_scaled, right))
                handed_on(last, last_in, after, 1, i).start()
                put(final, near(order[i]), -dot(handed, right))
                handed_on(final, final_in, after, 2, i).start()

    def take_update():
        send_update.wait_recv()

        @pl.when(t != parts - 1)
        def _():
            for j in range(ring):
                schur_ref[:, cell_columns(j)] -= update_in[j, :, lanes[0]].astype(jnp.float32)

    @pl.when(role == 2)
    def _():
        hand_fill.wait_recv()

    last_cells([0])

    @pl.when(inner)
    def _():
        ring_f.arrive(1)

    last_cells([1, 2])

    @pl.when(inner)
    def _():
        ring_f.arrive(2)

    take_update()
    last_cells([3, 4])

    @pl.when(inner)
    def _():
        ring_f.arrive(3)

    last_cells([5, 6])

    @pl.when(inner)
    def _():
        ring_f.arrive(4)

    last_cells([7])

    @pl.when(role == 3)
    def _():
        for i in range(ring):
            handed_on(far, far_in, before2, 0, i).wait_recv()
            handed_on(last, last_in, after, 1, i).wait_recv()
            handed_on(final, final_in, after, 2, i).wait_recv()
        for j in range(ring):
            at = cell_columns(j)
            schur_ref[:, at] -= last_in[j, :, lanes[0]].astype(jnp.float32)
            link_ref[:, at] = final_in[j, :, lanes[0]]

        @pl.when(t != parts - 1)
        def _():
            for j in range(ring):
                schur_ref[:, cell_columns(j)] -= far_in[j, :, lanes[0]].astype(jnp.float32)

    ring_a.drain()
    ring_w.drain()
    send_update.wait_send()
    for s in range(1, ring):
        spread_copy(diags, s, (d_send, d_recv)).wait_send()
    for k in range(3):
        returned(link_out, link_cells, k, 0, 2).wait_send()
        returned(form_out, form_cells, k, 1, -2).wait_send()
        returned(square_out, square_cells, k, 3, -2).wait_send()

    @pl.when(inner)
    def _():
        ring_f.drain()
        for k in range(3):
            returned(fill_out, fill_cells, k, 2, 2).wait_send()
        for s in range(1, ring):
            spread_copy(diags2, s, (d2_send, d2_recv)).wait_send()

    @pl.when(jnp.logical_not(inner))
    def _():
        for d in scaled_at:
            hand(d).wait_send()

    @pl.when(role == 1)
    def _():
        hand_fill.wait_send()
        for i in range(ring):
            handed_on(far, far_in, before2, 0, i).wait_send()

    @pl.when(role == 2)
    def _():
        for i in range(ring):
            handed_on(last, last_in, after, 1, i).wait_send()
            handed_on(final, final_in, after, 2, i).wait_send()


def solution(mesh):
    ring, parts = mesh.shape["space"], mesh.shape["tm"]

    def on_device(sep_block, own_couple, prev_couple, inner_diag):
        rows, width = sep_block.shape[1:]

        def block(kind, *lead):
            return pltpu.VMEM((*lead, rows, width), kind)

        def full(*lead):
            return pltpu.VMEM((*lead, width, width), jnp.bfloat16)

        line = pltpu.VMEM((1, width), jnp.float32)
        lines = pltpu.VMEM((ring, 1, width), jnp.float32)
        half = jnp.bfloat16
        dma = lambda count: pltpu.SemaphoreType.DMA((count,))
        hops = dma(4 * (ring // 2))

        def cells(count, parts_of):
            lanes = -(-parts_of * rows // 128) * 128
            return pltpu.VMEM((count, rows, lanes), half)

        schur, link = pl.pallas_call(
            functools.partial(kernel, ring, parts),
            out_shape=(
                jax.ShapeDtypeStruct((rows, width), jnp.float32),
                jax.ShapeDtypeStruct((rows, width), half),
            ),
            in_specs=[pl.BlockSpec(memory_space=pl.ANY)] * 3
            + [pl.BlockSpec(memory_space=pltpu.VMEM)],
            out_specs=(pl.BlockSpec(memory_space=pltpu.VMEM),) * 2,
            scratch_shapes=[
                block(jnp.float32), full(2), block(half, 2, 4), full(), block(half, 4), block(half, 4),
                full(), block(half), block(half),
                cells(ring, 1), cells(ring, 2), cells(ring, 1), cells(ring, 1),
                *[cells(ring, 1)] * 8,
                cells(3, 1), cells(3, 2), cells(3, 1), cells(3, 1),
                line, line, lines, line, line, lines,
                dma(3), hops, hops, hops, hops, hops, hops,
                dma(ring - 1), dma(ring - 1), dma(ring - 1), dma(ring - 1),
                dma(2), dma(2), dma(4), dma(4), dma(12), dma(12), dma(2), dma(2),
                dma(3 * ring), dma(3 * ring),
            ],
            compiler_params=pltpu.CompilerParams(
                collective_id=0, has_side_effects=True, vmem_limit_bytes=56 * 2**20
            ),
            cost_estimate=pl.CostEstimate(
                flops=7 * 2 * rows * width * width, bytes_accessed=10 * rows * width, transcendentals=0
            ),
        )(sep_block[0], own_couple[0], prev_couple[0], inner_diag)
        return schur[None], link[None]

    placed = (P("tm", "space", None), P("tm", "space", None), P("tm", "space", None), P("tm", None))
    return jax.shard_map(
        on_device,
        mesh=mesh,
        in_specs=placed,
        out_specs=(P("tm", "space", None), P("tm", "space", None)),
        check_vma=False,
    )
```

time: 192 us -> 150 us (0.78)
  Pallas kernels: 187 us -> 144 us
    pallas_call x1, Pallas kernels: 187 us -> 144 us  [on_device(): pl.pallas_call(functools.partial(kernel, ring, parts), out_shape=(jax.Sha...]
where the time goes in v2:
time: 150 us; the launch traced here: 148 us
  Pallas kernels  144 us (96%)
  local copies, waits for them, and re-layouts  3.24 us (2%)
    pallas_call x1, Pallas kernels, on_device(): pl.pallas_call(functools.partial(kernel, ring, parts), out_shape=(jax.Sha...  144 us
    unnamed x4, local copies, waits for them, and re-layouts  3.24 us

profile of v2, /device:TPU:11, one launch (start us, length us, event | category | flops | bytes accessed | tf_op | source)
XLA Modules:
  0.0 147.9 jit_solution(17871224098314707533)
XLA Ops:
  0.6 144.0 %shard_map.59 = (f32[192,1536]{1,0:T(8,128)}, bf16[192,1536]{1,0:T(8,128)(2,1)}) custom-call(f32[192,1536]{1,0:T(8,128)} %bitcast.7, bf16[192,1536]{1,0:T(8,128)(2,1)} %bitcast.8, bf16[192,1536]{1,0:T(8,128)(2,1)} %bitcast.9, f32[1,1536]{1,0:T(1,128)} %diag_ref.1), custom_call_target="tpu_custom_call" | custom-call | flops 6341787648 | bytes 2949120 | tf_op jit(solution)/shard_map/pallas_call | solution.py:523
  144.7 0.0 copy-start
  144.7 2.4 %copy.8 = f32[1,192,1536]{2,1,0:T(8,128)} copy(f32[1,192,1536]{2,1,0:T(8,128)} %bitcast.5) | data formatting | bytes 2359296
  147.1 0.0 copy-done
  147.1 0.8 copy.9
Async XLA Ops:
  144.7 2.4 %copy-start = (bf16[192,1536]{1,0:T(8,128)(2,1)S(1)}, bf16[192,1536]{1,0:T(8,128)(2,1)}, u32[]{:S(2)}) copy-start(bf16[192,1536]{1,0:T(8,128)(2,1)} %get-tuple-element.5) | copy-start | bytes 1769476

commit v3 on v0

v3 whole, which is shorter than its diff:
```python
import functools

import jax
import jax.numpy as jnp
from jax import lax
from jax.experimental import pallas as pl
from jax.experimental.pallas import tpu as pltpu
from jax.sharding import PartitionSpec as P

MESH = pl.DeviceIdType.MESH
OWN, PREV = 0, 1


def kernel(
    ring, parts, sep_hbm, own_hbm, prev_hbm, diag_ref, schur_ref, link_ref,
    sep, pair, scaled, link, link_scaled, sibling, turned, fill_scaled, handed,
    passed, passed_in, last, last_in, left, left_wide, far_left,
    link_cells, form_cells, fill_cells, square_cells, final_cells, update_in,
    reciprocal, edge, edge_in, diags, edge2, edge2_in, diags2,
    load_sem, y_send, y_recv, x_send, x_recv,
    d_send, d_recv, d2_send, d2_recv, e_send, e_recv, m_send, m_recv, t_send, t_recv, go,
):
    rows, width = sep.shape
    chunk = 16
    tile = 512
    z = lax.axis_index("space")
    t = lax.axis_index("tm")
    odd = lax.rem(t, 2)
    role = lax.rem(t, 4)
    is_odd = odd == 1
    inner = jnp.logical_or(role == 1, role == 2)
    outer = jnp.logical_not(inner)
    sib = t + 1 - 2 * odd
    across = lax.rem(t + 2 * odd - 1 + parts, parts)
    before = lax.rem(t + parts - 1, parts)
    after = lax.rem(t + 1, parts)
    first, second = 1 - odd, odd

    barrier = pltpu.get_barrier_semaphore()
    for k in range(1, ring):
        pl.semaphore_signal(
            barrier, inc=1, device_id={"space": lax.rem(z + k, ring)}, device_id_type=MESH
        )
    for peer in (before, after):
        pl.semaphore_signal(barrier, inc=1, device_id={"tm": peer}, device_id_type=MESH)

    def near(d):
        return lax.rem(z + d + ring, ring)

    def row_slice(d):
        return pl.ds(pl.multiple_of(near(d) * rows, rows), rows)

    def cell_columns(j):
        return slice(j * rows, (j + 1) * rows)

    loads = [
        pltpu.make_async_copy(own_hbm, pair.at[OWN, row_slice(0)], load_sem.at[0]),
        pltpu.make_async_copy(prev_hbm, pair.at[PREV, row_slice(0)], load_sem.at[1]),
        pltpu.make_async_copy(sep_hbm, sep, load_sem.at[2]),
    ]
    for load in loads:
        load.start()
    for load in loads:
        load.wait()
    pl.semaphore_wait(barrier, ring + 1)

    def along(src, dst, way, send_sem, recv_sem):
        return pltpu.make_async_remote_copy(
            src_ref=src, dst_ref=dst, send_sem=send_sem, recv_sem=recv_sem,
            device_id={"space": near(way)}, device_id_type=MESH,
        )

    def to_part(src, dst, peer, send_sem, recv_sem):
        return pltpu.make_async_remote_copy(
            src_ref=src, dst_ref=dst, send_sem=send_sem, recv_sem=recv_sem,
            device_id={"tm": peer}, device_id_type=MESH,
        )

    class Ring:
        def __init__(self, buf, pieces, send_sem, recv_sem):
            size = rows // pieces
            self.streams = []
            for i in range(pieces):
                long_way = 1 if i % 2 == 0 else -1
                self.streams.append((buf, i * size, size, long_way, ring // 2))
                self.streams.append((buf, i * size, size, -long_way, ring // 2 - 1))
            self.sems = send_sem, recv_sem

        def at(self, s, step):
            buf, offset, count, way, _ = self.streams[s]
            at = s * (ring // 2) + step - 1
            slot = near(-way * (step - 1))
            piece = buf.at[pl.ds(pl.multiple_of(slot * rows + offset, chunk), count)]
            return along(piece, piece, way, self.sems[0].at[at], self.sems[1].at[at])

        def start(self, begin=0, end=None):
            for s in range(len(self.streams))[begin:end]:
                self.at(s, 1).start()

        def arrive(self, step):
            for s, stream in enumerate(self.streams):
                if step <= stream[4]:
                    self.at(s, step).wait_recv()
                    if step < stream[4]:
                        self.at(s, step + 1).start()

        def drain(self):
            for s, stream in enumerate(self.streams):
                for step in range(1, stream[4] + 1):
                    self.at(s, step).wait_send()

    x_all = pair.at[first]
    y_all = pair.at[second]
    ring_y = Ring(y_all, 2, y_send, y_recv)
    ring_x = Ring(x_all, 4, x_send, x_recv)
    ring_y.start()

    def diag_part(out, sep_factor, terms):
        out[...] = jnp.zeros_like(out)

        @pl.loop(0, rows // chunk)
        def _(i):
            at = pl.multiple_of(i * chunk, chunk)
            total = jnp.zeros((chunk, 1), jnp.float32)
            for left_rows, right_rows in terms:
                total += jnp.sum(
                    left_rows[pl.ds(at, chunk), :].astype(jnp.float32)
                    * right_rows[pl.ds(at, chunk), :].astype(jnp.float32),
                    axis=1, keepdims=True,
                )
            spot = lax.broadcasted_iota(jnp.int32, (chunk, width), 1) == (
                lax.broadcasted_iota(jnp.int32, (chunk, width), 0) + (z * rows + at)
            )
            values = sep[pl.ds(at, chunk), :] * sep_factor - total
            out[...] += jnp.sum(jnp.where(spot, values, 0.0), axis=0, keepdims=True)

    def edge_copy(edge, edge_in, peer, k):
        return to_part(edge, edge_in, peer, e_send.at[k], e_recv.at[k])

    def spread_copy(diags, s, sems):
        return along(diags.at[z], diags.at[z], s, sems[0].at[s - 1], sems[1].at[s - 1])

    def spread(edge, edge_in, diags, peer, k, sems):
        edge_copy(edge, edge_in, peer, k).wait()
        diags[z] = edge[...] + edge_in[...]
        for s in range(1, ring):
            spread_copy(diags, s, sems).start()

    def pivot_scale(diags, sems):
        for s in range(1, ring):
            spread_copy(diags, s, sems).wait_recv()
        values = diags[0]
        for s in range(1, ring):
            values += diags[s]
        return (1.0 / jnp.maximum(values, 1.0)).astype(jnp.bfloat16).astype(jnp.float32)

    def scale_rows(source, factors, out):
        @pl.loop(0, rows // chunk)
        def _(i):
            at = pl.ds(pl.multiple_of(i * chunk, chunk), chunk)
            out[at, :] = (source[at, :].astype(jnp.float32) * factors).astype(jnp.bfloat16)

    def dot(left_rows, right_rows):
        return lax.dot_general(
            left_rows[...], right_rows[...], (((1,), (1,)), ((), ())),
            preferred_element_type=jnp.float32,
        )

    def times(left_rows, matrix, take):
        @pl.loop(0, width // tile)
        def _(j):
            at = pl.ds(pl.multiple_of(j * tile, tile), tile)
            take(at, jnp.dot(left_rows[...], matrix[:, at], preferred_element_type=jnp.float32))

    def times_turned(left_rows, matrix, take):
        @pl.loop(0, width // tile)
        def _(j):
            at = pl.ds(pl.multiple_of(j * tile, tile), tile)
            take(at, dot(left_rows, matrix.at[at]))

    def scaled_into(out, factors):
        def take(at, value):
            out[:, at] = (value * factors[:, at]).astype(jnp.bfloat16)

        return take

    cell = slice(0, rows)

    def put(cells, d, value):
        cells[near(d), :, cell] = value.astype(jnp.bfloat16)

    def x_rows(d):
        return x_all.at[row_slice(d)]

    def y_rows(d):
        return y_all.at[row_slice(d)]

    reach = {0: (0,), 4: (ring // 2,)}
    for step in range(1, ring // 2):
        reach[step] = (-step, step)

    reciprocal[...] = 1.0 / diag_ref[...]
    x_scaled, y_scaled = scaled.at[0], scaled.at[1]
    scale_rows(y_rows(0), reciprocal[...], y_scaled)
    scale_rows(x_rows(0), reciprocal[...], x_scaled)
    diag_part(edge, (1 - odd).astype(jnp.float32), [(y_scaled, y_rows(0))])
    edge_copy(edge, edge_in, sib, 0).start()
    spread(edge, edge_in, diags, sib, 0, (d_send, d_recv))

    sign = jnp.where(t == 0, 0.0, -1.0)

    def link_and_form(step):
        for d in reach[step]:
            put(link_cells, d, dot(x_scaled, y_rows(d)) * sign)
            put(form_cells, d, dot(y_scaled, y_rows(d)))

    link_and_form(0)
    for step in (1, 2, 3):
        ring_y.arrive(step)
        if step == 3:

            @pl.when(inner)
            def _():
                ring_x.start(0, 2)

        link_and_form(step)
    ring_y.arrive(4)

    @pl.when(inner)
    def _():
        ring_x.start(2)

    link_and_form(4)
    for j in range(ring):
        link[:, cell_columns(j)] = link_cells[j, :, cell]
    scale1 = edge
    scale1[...] = pivot_scale(diags, (d_send, d_recv))
    scale_rows(link, scale1[...], link_scaled)

    hand_link = to_part(link_scaled, sibling, sib, m_send.at[0], m_recv.at[0])
    hand_back = to_part(passed, passed_in, sib, m_send.at[1], m_recv.at[1])
    hand_last = to_part(last, last_in, sib, m_send.at[2], m_recv.at[2])
    hand_fill = to_part(fill_scaled, handed, after, m_send.at[3], m_recv.at[3])
    send_form = to_part(form_cells, update_in, before, m_send.at[4], m_recv.at[4])
    send_square = to_part(square_cells, update_in, before, m_send.at[4], m_recv.at[4])

    @pl.when(outer)
    def _():
        hand_link.start()

    @pl.when(is_odd)
    def _():
        send_form.start()

    def take_left(at, value):
        left_wide[:, at] = x_scaled[:, at].astype(jnp.float32) - value * reciprocal[:, at]

    def round_left():
        left[...] = left_wide[...].astype(jnp.bfloat16)

    def square_cell(step):
        for d in reach[step]:
            put(square_cells, d, dot(left, x_rows(d)))

    def even_result():
        send_form.wait_recv()
        for j in range(ring):
            at = cell_columns(j)
            taken = form_cells[j, :, cell].astype(jnp.float32)
            taken += update_in[j, :, cell].astype(jnp.float32)
            schur_ref[:, at] = sep[:, at] - taken
        link_ref[...] = link[...]

    @pl.when(inner)
    def _():
        diag_part(
            edge2, odd.astype(jnp.float32), [(x_scaled, x_rows(0)), (link_scaled, link)]
        )
        edge_copy(edge2, edge2_in, across, 1).start()
        times(link_scaled, y_all, take_left)
        round_left()
        ring_x.arrive(1)
        hand_link.wait_recv()
        times(sibling, y_all, scaled_into(turned, reciprocal))
        spread(edge2, edge2_in, diags2, across, 1, (d2_send, d2_recv))

        def fill_cell(step):
            for d in reach[step]:
                put(fill_cells, d, dot(turned, x_rows(d)))

        fill_cell(0)
        fill_cell(1)
        ring_x.arrive(2)
        fill_cell(2)
        square_cell(0)
        square_cell(1)
        ring_x.arrive(3)
        pl.semaphore_signal(go, inc=1, device_id={"tm": sib}, device_id_type=MESH)
        fill_cell(3)
        edge2[...] = pivot_scale(diags2, (d2_send, d2_recv))
        ring_x.arrive(4)
        fill_cell(4)
        for j in range(ring):
            turned[:, cell_columns(j)] = fill_cells[j, :, cell]
        scale_rows(turned, edge2[...], fill_scaled)

        @pl.when(role == 1)
        def _():
            hand_fill.start()

        times(fill_scaled, x_all, scaled_into(sibling, reciprocal))
        times_turned(sibling, y_all, scaled_into(passed, scale1))
        hand_back.start()
        square_cell(2)
        square_cell(3)
        square_cell(4)

        @pl.when(role == 2)
        def _():
            send_square.start()
            hand_fill.wait_recv()
            times(handed, x_all, scaled_into(sibling, reciprocal))
            times_turned(sibling, y_all, scaled_into(last, scale1))
            hand_last.start()
            even_result()

        @pl.when(role == 1)
        def _():
            link_ref[...] = turned[...]
            send_square.wait_recv()
            for j in range(ring):
                at = cell_columns(j)
                taken = square_cells[j, :, cell].astype(jnp.float32)
                taken += update_in[j, :, cell].astype(jnp.float32)
                schur_ref[:, at] = sep[:, at] - taken

    order = [d for step in range(ring // 2 + 1) for d in reach[step]]

    def send_cell(d):
        i = order.index(d)
        cells = square_cells.at[near(d)]
        return to_part(cells, update_in.at[near(d)], before, t_send.at[i], t_recv.at[i])

    @pl.when(outer)
    def _():
        times(link_scaled, y_all, take_left)

        @pl.when(role == 0)
        def _():
            even_result()

        pl.semaphore_wait(go, 1)
        ring_x.start()

        def outer_cells(step):
            square_cell(step)

            @pl.when(role == 0)
            def _():
                for d in reach[step]:
                    send_cell(d).start()

        def final_cell(step):
            for d in reach[step]:
                put(final_cells, d, dot(far_left, x_rows(d)))

        ring_x.arrive(1)
        ring_x.arrive(2)
        hand_back.wait_recv()

        def take_more(at, value):
            left_wide[:, at] -= value * reciprocal[:, at]

        times(passed_in, y_all, take_more)
        round_left()
        outer_cells(0)
        outer_cells(1)
        outer_cells(2)
        ring_x.arrive(3)
        outer_cells(3)

        @pl.when(role == 3)
        def _():
            hand_last.wait_recv()
            times(last_in, y_all, scaled_into(far_left, reciprocal))
            for step in range(4):
                final_cell(step)

        ring_x.arrive(4)
        outer_cells(4)

        @pl.when(role == 3)
        def _():
            final_cell(4)
            for j in range(ring):
                at = cell_columns(j)
                schur_ref[:, at] = sep[:, at] - square_cells[j, :, cell].astype(jnp.float32)
                link_ref[:, at] = final_cells[j, :, cell]
            for d in order:
                send_cell(d).wait_recv()

            @pl.when(t != parts - 1)
            def _():
                for j in range(ring):
                    schur_ref[:, cell_columns(j)] -= update_in[j, :, cell].astype(jnp.float32)

    ring_y.drain()
    ring_x.drain()
    for s in range(1, ring):
        spread_copy(diags, s, (d_send, d_recv)).wait_send()

    @pl.when(inner)
    def _():
        hand_back.wait_send()
        for s in range(1, ring):
            spread_copy(diags2, s, (d2_send, d2_recv)).wait_send()

    @pl.when(outer)
    def _():
        hand_link.wait_send()

    @pl.when(is_odd)
    def _():
        send_form.wait_send()

    @pl.when(role == 0)
    def _():
        for d in order:
            send_cell(d).wait_send()

    @pl.when(role == 1)
    def _():
        hand_fill.wait_send()

    @pl.when(role == 2)
    def _():
        send_square.wait_send()
        hand_last.wait_send()


def solution(mesh):
    ring, parts = mesh.shape["space"], mesh.shape["tm"]

    def on_device(sep_block, own_couple, prev_couple, inner_diag):
        rows, width = sep_block.shape[1:]

        def block(kind, *lead):
            return pltpu.VMEM((*lead, rows, width), kind)

        def full(*lead):
            return pltpu.VMEM((*lead, width, width), jnp.bfloat16)

        line = pltpu.VMEM((1, width), jnp.float32)
        lines = pltpu.VMEM((ring, 1, width), jnp.float32)
        half = jnp.bfloat16
        dma = lambda count: pltpu.SemaphoreType.DMA((count,))
        cells = pltpu.VMEM((ring, rows, -(-rows // 128) * 128), half)
        schur, link = pl.pallas_call(
            functools.partial(kernel, ring, parts),
            out_shape=(
                jax.ShapeDtypeStruct((rows, width), jnp.float32),
                jax.ShapeDtypeStruct((rows, width), half),
            ),
            in_specs=[pl.BlockSpec(memory_space=pl.ANY)] * 3
            + [pl.BlockSpec(memory_space=pltpu.VMEM)],
            out_specs=(pl.BlockSpec(memory_space=pltpu.VMEM),) * 2,
            scratch_shapes=[
                block(jnp.float32), full(2), block(half, 2), *[block(half)] * 10,
                block(half), block(jnp.float32), block(half), *[cells] * 6,
                line, line, line, lines, line, line, lines,
                dma(3), dma(2 * ring), dma(2 * ring), dma(4 * ring), dma(4 * ring),
                dma(ring - 1), dma(ring - 1), dma(ring - 1), dma(ring - 1),
                dma(2), dma(2), dma(5), dma(5), dma(ring), dma(ring), pltpu.SemaphoreType.REGULAR,
            ],
            compiler_params=pltpu.CompilerParams(
                collective_id=0, has_side_effects=True, vmem_limit_bytes=56 * 2**20
            ),
            cost_estimate=pl.CostEstimate(
                flops=7 * 2 * rows * width * width, bytes_accessed=10 * rows * width, transcendentals=0
            ),
        )(sep_block[0], own_couple[0], prev_couple[0], inner_diag)
        return schur[None], link[None]

    placed = (P("tm", "space", None), P("tm", "space", None), P("tm", "space", None), P("tm", None))
    return jax.shard_map(
        on_device,
        mesh=mesh,
        in_specs=placed,
        out_specs=(P("tm", "space", None), P("tm", "space", None)),
        check_vma=False,
    )
```

time: 521 us -> 113 us (0.22); the launches traced: 514 us -> 113 us
  waiting for transfers between devices: 398 us -> 0 us
  Pallas kernels: 0 us -> 109 us
  matrix products: 39.4 us -> 0 us
  starting transfers between devices: 28 us -> 0 us
  blocking collectives: 23.6 us -> 0 us
  between operations: 14.6 us -> 0.65 us
    all_gather x3 -> x0, waiting for transfers between devices: 228 us -> none  [the longest x2 121 us: reduce_level(): own_full = lax.all_gather(link, 'space', axis=0, tiled=True)]
    ppermute x9 -> x0, waiting for transfers between devices: 170 us -> none  [passed_along(): return lax.ppermute(block, axis, route)]
    pallas_call x0 -> x1, Pallas kernels: none -> 109 us  [on_device(): pl.pallas_call(functools.partial(kernel, ring, parts), out_shape=(jax.Sha...]
    dot_general x9 -> x0, matrix products: 39.4 us -> none  [the longest x5 23.8 us: outer_form(): jnp.einsum('ik,jk->ij', left_side, right_side, preferred_element_type=jnp...]
    ppermute x9 -> x0, starting transfers between devices: 27.9 us -> none  [passed_along(): return lax.ppermute(block, axis, route)]
    unnamed x2 -> x0, blocking collectives: 23.6 us -> none
  transfers between devices with their start and end apart: 12 -> 0, of which waited for: 8 -> 0; matrix products, arithmetic and copies ran while one was open for 5% -> 0% of each run, Pallas kernels for 0% -> 0%
where the time goes in v3:
time: 113 us
  Pallas kernels  109 us (96%)
  local copies, waits for them, and re-layouts  3.24 us (3%)
    pallas_call x1, Pallas kernels, on_device(): pl.pallas_call(functools.partial(kernel, ring, parts), out_shape=(jax.Sha...  109 us
    unnamed x4, local copies, waits for them, and re-layouts  3.24 us

profile of v3, /device:TPU:11, one launch (start us, length us, event | category | flops | bytes accessed | tf_op | source)
XLA Modules:
  0.0 112.6 jit_solution(16959239182393994663)
XLA Ops:
  0.6 108.7 %shard_map.59 = (f32[192,1536]{1,0:T(8,128)}, bf16[192,1536]{1,0:T(8,128)(2,1)}) custom-call(f32[192,1536]{1,0:T(8,128)} %bitcast.7, bf16[192,1536]{1,0:T(8,128)(2,1)} %bitcast.8, bf16[192,1536]{1,0:T(8,128)(2,1)} %bitcast.9, f32[1,1536]{1,0:T(1,128)} %diag_ref.1), custom_call_target="tpu_custom_call" | custom-call | flops 6341787648 | bytes 2949120 | tf_op jit(solution)/shard_map/pallas_call | solution.py:458
  109.4 0.0 copy-start
  109.4 2.4 %copy.8 = f32[1,192,1536]{2,1,0:T(8,128)} copy(f32[1,192,1536]{2,1,0:T(8,128)} %bitcast.5) | data formatting | bytes 2359296
  111.8 0.0 copy-done
  111.8 0.8 copy.9
Async XLA Ops:
  109.4 2.4 %copy-start = (bf16[192,1536]{1,0:T(8,128)(2,1)S(1)}, bf16[192,1536]{1,0:T(8,128)(2,1)}, u32[]{:S(2)}) copy-start(bf16[192,1536]{1,0:T(8,128)(2,1)} %get-tuple-element.5) | copy-start | bytes 1769476

commit v4 on v3

--- a/solution.py
+++ b/solution.py
@@ -268,7 +268,7 @@
             at = cell_columns(j)
             taken = form_cells[j, :, cell].astype(jnp.float32)
             taken += update_in[j, :, cell].astype(jnp.float32)
-            schur_ref[:, at] = sep[:, at] - taken
+            schur_ref[:, at] = taken.astype(jnp.bfloat16)
         link_ref[...] = link[...]
 
     @pl.when(inner)
@@ -332,7 +332,7 @@
                 at = cell_columns(j)
                 taken = square_cells[j, :, cell].astype(jnp.float32)
                 taken += update_in[j, :, cell].astype(jnp.float32)
-                schur_ref[:, at] = sep[:, at] - taken
+                schur_ref[:, at] = taken.astype(jnp.bfloat16)
 
     order = [d for step in range(ring // 2 + 1) for d in reach[step]]
 
@@ -394,7 +394,7 @@
             final_cell(4)
             for j in range(ring):
                 at = cell_columns(j)
-                schur_ref[:, at] = sep[:, at] - square_cells[j, :, cell].astype(jnp.float32)
+                schur_ref[:, at] = square_cells[j, :, cell]
                 link_ref[:, at] = final_cells[j, :, cell]
             for d in order:
                 send_cell(d).wait_recv()
@@ -402,7 +402,10 @@
             @pl.when(t != parts - 1)
             def _():
                 for j in range(ring):
-                    schur_ref[:, cell_columns(j)] -= update_in[j, :, cell].astype(jnp.float32)
+                    at = cell_columns(j)
+                    taken = square_cells[j, :, cell].astype(jnp.float32)
+                    taken += update_in[j, :, cell].astype(jnp.float32)
+                    schur_ref[:, at] = taken.astype(jnp.bfloat16)
 
     ring_y.drain()
     ring_x.drain()
@@ -436,6 +439,28 @@
     def _():
         send_square.wait_send()
         hand_last.wait_send()
+
+
+def finish(sep_in, taken_in, link_in, schur_out, link_out, sep, taken, link, sems):
+    count = 4
+    step = sep_in.shape[0] // count
+    slabs = [pl.ds(i * step, step) for i in range(count)]
+    loads, stores = [], []
+    for i, at in enumerate(slabs):
+        for k, (src, dst) in enumerate(((sep_in, sep), (taken_in, taken), (link_in, link))):
+            copy = pltpu.make_async_copy(src.at[at], dst.at[at], sems.at[k, i])
+            copy.start()
+            loads.append(copy)
+    for i, at in enumerate(slabs):
+        for k in range(3):
+            loads[3 * i + k].wait()
+        sep[at, :] -= taken[at, :].astype(jnp.float32)
+        for k, (src, dst) in enumerate(((sep, schur_out), (link, link_out))):
+            copy = pltpu.make_async_copy(src.at[at], dst.at[at], sems.at[3 + k, i])
+            copy.start()
+            stores.append(copy)
+    for copy in stores:
+        copy.wait()
 
 
 def solution(mesh):
@@ -455,10 +480,10 @@
         half = jnp.bfloat16
         dma = lambda count: pltpu.SemaphoreType.DMA((count,))
         cells = pltpu.VMEM((ring, rows, -(-rows // 128) * 128), half)
-        schur, link = pl.pallas_call(
+        taken, link = pl.pallas_call(
             functools.partial(kernel, ring, parts),
             out_shape=(
-                jax.ShapeDtypeStruct((rows, width), jnp.float32),
+                jax.ShapeDtypeStruct((rows, width), half),
                 jax.ShapeDtypeStruct((rows, width), half),
             ),
             in_specs=[pl.BlockSpec(memory_space=pl.ANY)] * 3
@@ -473,12 +498,25 @@
                 dma(2), dma(2), dma(5), dma(5), dma(ring), dma(ring), pltpu.SemaphoreType.REGULAR,
             ],
             compiler_params=pltpu.CompilerParams(
-                collective_id=0, has_side_effects=True, vmem_limit_bytes=56 * 2**20
+                collective_id=0, has_side_effects=True, vmem_limit_bytes=63 * 2**20
             ),
             cost_estimate=pl.CostEstimate(
                 flops=7 * 2 * rows * width * width, bytes_accessed=10 * rows * width, transcendentals=0
             ),
         )(sep_block[0], own_couple[0], prev_couple[0], inner_diag)
+        schur, link = pl.pallas_call(
+            finish,
+            out_shape=(
+                jax.ShapeDtypeStruct((rows, width), jnp.float32),
+                jax.ShapeDtypeStruct((rows, width), half),
+            ),
+            in_specs=[pl.BlockSpec(memory_space=pl.ANY)] * 3,
+            out_specs=(pl.BlockSpec(memory_space=pl.ANY),) * 2,
+            scratch_shapes=[
+                block(jnp.float32), block(half), block(half), pltpu.SemaphoreType.DMA((5, 4))
+            ],
+            compiler_params=pltpu.CompilerParams(vmem_limit_bytes=60 * 2**20),
+        )(sep_block[0], taken, link)
         return schur[None], link[None]
 
     placed = (P("tm", "space", None), P("tm", "space", None), P("tm", "space", None), P("tm", None))

time: 113 us -> 112 us (level)
  local copies, waits for them, and re-layouts: 3.24 us -> 0 us
  Pallas kernels: 109 us -> 111 us
    unnamed x4 -> x0, local copies, waits for them, and re-layouts: 3.24 us -> none
    pallas_call x0 -> x1, Pallas kernels: none -> 2.59 us  [on_device(): pl.pallas_call(finish, out_shape=(jax.ShapeDtypeStruct((rows, width), jnp...]
where the time goes in v4:
time: 112 us
  Pallas kernels  111 us (99%)
    pallas_call x1, Pallas kernels, on_device(): pl.pallas_call(functools.partial(kernel, ring, parts), out_shape=(jax.Sha...  109 us
    pallas_call x1, Pallas kernels, on_device(): pl.pallas_call(finish, out_shape=(jax.ShapeDtypeStruct((rows, width), jnp...  2.59 us

profile of v4, /device:TPU:11, one launch (start us, length us, event | category | flops | bytes accessed | tf_op | source)
XLA Modules:
  0.0 111.7 jit_solution(5915551920931486945)
XLA Ops:
  0.6 108.5 %shard_map.59 = (bf16[192,1536]{1,0:T(8,128)(2,1)}, bf16[192,1536]{1,0:T(8,128)(2,1)}) custom-call(f32[192,1536]{1,0:T(8,128)} %bitcast.5, bf16[192,1536]{1,0:T(8,128)(2,1)} %bitcast.8, bf16[192,1536]{1,0:T(8,128)(2,1)} %bitcast.9, f32[1,1536]{1,0:T(1,128)} %diag_ref.1), custom_call_target="tpu_custom_call" | custom-call | flops 6341787648 | bytes 2949120 | tf_op jit(solution)/shard_map/pallas_call | solution.py:483
  109.2 2.6 %shard_map.60 = (f32[192,1536]{1,0:T(8,128)}, bf16[192,1536]{1,0:T(8,128)(2,1)}) custom-call(f32[192,1536]{1,0:T(8,128)} %bitcast.6, bf16[192,1536]{1,0:T(8,128)(2,1)} %get-tuple-element.6.taken_in, bf16[192,1536]{1,0:T(8,128)(2,1)} %get-tuple-element.7.link_in), custom_call_target="tpu_custom_call" | custom-call | tf_op jit(solution)/shard_map/pallas_call | solution.py:507

commit v5 on v4

--- a/solution.py
+++ b/solution.py
@@ -137,8 +137,12 @@
     def edge_copy(edge, edge_in, peer, k):
         return to_part(edge, edge_in, peer, e_send.at[k], e_recv.at[k])
 
+    span = 2 * rows
+    my_span = pl.ds(pl.multiple_of(lax.div(z, 2) * span, span), span)
+
     def spread_copy(diags, s, sems):
-        return along(diags.at[z], diags.at[z], s, sems[0].at[s - 1], sems[1].at[s - 1])
+        mine = diags.at[z, :, my_span]
+        return along(mine, mine, s, sems[0].at[s - 1], sems[1].at[s - 1])
 
     def spread(edge, edge_in, diags, peer, k, sems):
         edge_copy(edge, edge_in, peer, k).wait()
@@ -146,13 +150,14 @@
         for s in range(1, ring):
             spread_copy(diags, s, sems).start()
 
-    def pivot_scale(diags, sems):
+    def pivot_scale(diags, sems, out):
         for s in range(1, ring):
             spread_copy(diags, s, sems).wait_recv()
-        values = diags[0]
-        for s in range(1, ring):
-            values += diags[s]
-        return (1.0 / jnp.maximum(values, 1.0)).astype(jnp.bfloat16).astype(jnp.float32)
+        for k in range(ring // 2):
+            at = slice(k * span, (k + 1) * span)
+            values = diags[2 * k, :, at] + diags[2 * k + 1, :, at]
+            scale = (1.0 / jnp.maximum(values, 1.0)).astype(jnp.bfloat16)
+            out[:, at] = scale.astype(jnp.float32)
 
     def scale_rows(source, factors, out):
         @pl.loop(0, rows // chunk)
@@ -234,7 +239,7 @@
     for j in range(ring):
         link[:, cell_columns(j)] = link_cells[j, :, cell]
     scale1 = edge
-    scale1[...] = pivot_scale(diags, (d_send, d_recv))
+    pivot_scale(diags, (d_send, d_recv), scale1)
     scale_rows(link, scale1[...], link_scaled)
 
     hand_link = to_part(link_scaled, sibling, sib, m_send.at[0], m_recv.at[0])
@@ -297,7 +302,7 @@
         ring_x.arrive(3)
         pl.semaphore_signal(go, inc=1, device_id={"tm": sib}, device_id_type=MESH)
         fill_cell(3)
-        edge2[...] = pivot_scale(diags2, (d2_send, d2_recv))
+        pivot_scale(diags2, (d2_send, d2_recv), edge2)
         ring_x.arrive(4)
         fill_cell(4)
         for j in range(ring):

time: 112 us -> 111 us (level)
    pallas_call x1, Pallas kernels: 109 us -> 107 us  [on_device(): pl.pallas_call(functools.partial(kernel, ring, parts), out_shape=(jax.Sha...]
where the time goes in v5:
time: 111 us
  Pallas kernels  110 us (99%)
    pallas_call x1, Pallas kernels, on_device(): pl.pallas_call(functools.partial(kernel, ring, parts), out_shape=(jax.Sha...  107 us
    pallas_call x1, Pallas kernels, on_device(): pl.pallas_call(finish, out_shape=(jax.ShapeDtypeStruct((rows, width), jnp...  2.59 us

profile of v5, /device:TPU:11, one launch (start us, length us, event | category | flops | bytes accessed | tf_op | source)
XLA Modules:
  0.0 110.6 jit_solution(17233684989476739948)
XLA Ops:
  0.6 107.3 %shard_map.59 = (bf16[192,1536]{1,0:T(8,128)(2,1)}, bf16[192,1536]{1,0:T(8,128)(2,1)}) custom-call(f32[192,1536]{1,0:T(8,128)} %bitcast.5, bf16[192,1536]{1,0:T(8,128)(2,1)} %bitcast.8, bf16[192,1536]{1,0:T(8,128)(2,1)} %bitcast.9, f32[1,1536]{1,0:T(1,128)} %diag_ref.1), custom_call_target="tpu_custom_call" | custom-call | flops 6341787648 | bytes 2949120 | tf_op jit(solution)/shard_map/pallas_call | solution.py:488
  108.0 2.6 %shard_map.60 = (f32[192,1536]{1,0:T(8,128)}, bf16[192,1536]{1,0:T(8,128)(2,1)}) custom-call(f32[192,1536]{1,0:T(8,128)} %bitcast.6, bf16[192,1536]{1,0:T(8,128)(2,1)} %get-tuple-element.6.taken_in, bf16[192,1536]{1,0:T(8,128)(2,1)} %get-tuple-element.7.link_in), custom_call_target="tpu_custom_call" | custom-call | tf_op jit(solution)/shard_map/pallas_call | solution.py:512

commit v6 on v5

--- a/solution.py
+++ b/solution.py
@@ -60,8 +60,6 @@
     ]
     for load in loads:
         load.start()
-    for load in loads:
-        load.wait()
     pl.semaphore_wait(barrier, ring + 1)
 
     def along(src, dst, way, send_sem, recv_sem):
@@ -97,6 +95,15 @@
             for s in range(len(self.streams))[begin:end]:
                 self.at(s, 1).start()
 
+        def start_from(self, source):
+            for s, (buf, offset, count, way, _) in enumerate(self.streams):
+                at = s * (ring // 2)
+                piece = buf.at[pl.ds(pl.multiple_of(near(0) * rows + offset, chunk), count)]
+                along(
+                    source.at[pl.ds(offset, count)], piece, way,
+                    self.sems[0].at[at], self.sems[1].at[at],
+                ).start()
+
         def arrive(self, step):
             for s, stream in enumerate(self.streams):
                 if step <= stream[4]:
@@ -113,7 +120,17 @@
     y_all = pair.at[second]
     ring_y = Ring(y_all, 2, y_send, y_recv)
     ring_x = Ring(x_all, 4, x_send, x_recv)
-    ring_y.start()
+
+    @pl.when(is_odd)
+    def _():
+        ring_y.start_from(prev_hbm)
+
+    @pl.when(jnp.logical_not(is_odd))
+    def _():
+        ring_y.start_from(own_hbm)
+
+    for load in loads[:2]:
+        load.wait()
 
     def diag_part(out, sep_factor, terms):
         out[...] = jnp.zeros_like(out)
@@ -208,6 +225,7 @@
     x_scaled, y_scaled = scaled.at[0], scaled.at[1]
     scale_rows(y_rows(0), reciprocal[...], y_scaled)
     scale_rows(x_rows(0), reciprocal[...], x_scaled)
+    loads[2].wait()
     diag_part(edge, (1 - odd).astype(jnp.float32), [(y_scaled, y_rows(0))])
     edge_copy(edge, edge_in, sib, 0).start()
     spread(edge, edge_in, diags, sib, 0, (d_send, d_recv))
@@ -447,7 +465,7 @@
 
 
 def finish(sep_in, taken_in, link_in, schur_out, link_out, sep, taken, link, sems):
-    count = 4
+    count = 6
     step = sep_in.shape[0] // count
     slabs = [pl.ds(i * step, step) for i in range(count)]
     loads, stores = [], []
@@ -518,7 +536,7 @@
             in_specs=[pl.BlockSpec(memory_space=pl.ANY)] * 3,
             out_specs=(pl.BlockSpec(memory_space=pl.ANY),) * 2,
             scratch_shapes=[
-                block(jnp.float32), block(half), block(half), pltpu.SemaphoreType.DMA((5, 4))
+                block(jnp.float32), block(half), block(half), pltpu.SemaphoreType.DMA((5, 6))
             ],
             compiler_params=pltpu.CompilerParams(vmem_limit_bytes=60 * 2**20),
         )(sep_block[0], taken, link)

time: 111 us -> 111 us (level)
  no operation moved by 1% of the time
where the time goes in v6:
time: 111 us
  Pallas kernels  110 us (99%)
    pallas_call x1, Pallas kernels, on_device(): pl.pallas_call(functools.partial(kernel, ring, parts), out_shape=(jax.Sha...  108 us
    pallas_call x1, Pallas kernels, on_device(): pl.pallas_call(finish, out_shape=(jax.ShapeDtypeStruct((rows, width), jnp...  2.68 us

profile of v6, /device:TPU:11, one launch (start us, length us, event | category | flops | bytes accessed | tf_op | source)
XLA Modules:
  0.0 110.9 jit_solution(11635151770860699720)
XLA Ops:
  0.6 107.6 %shard_map.59 = (bf16[192,1536]{1,0:T(8,128)(2,1)}, bf16[192,1536]{1,0:T(8,128)(2,1)}) custom-call(f32[192,1536]{1,0:T(8,128)} %bitcast.5, bf16[192,1536]{1,0:T(8,128)(2,1)} %bitcast.8, bf16[192,1536]{1,0:T(8,128)(2,1)} %bitcast.9, f32[1,1536]{1,0:T(1,128)} %diag_ref.1), custom_call_target="tpu_custom_call" | custom-call | flops 6341787648 | bytes 2949120 | tf_op jit(solution)/shard_map/pallas_call | solution.py:506
  108.2 2.7 %shard_map.60 = (f32[192,1536]{1,0:T(8,128)}, bf16[192,1536]{1,0:T(8,128)(2,1)}) custom-call(f32[192,1536]{1,0:T(8,128)} %bitcast.6, bf16[192,1536]{1,0:T(8,128)(2,1)} %get-tuple-element.6.taken_in, bf16[192,1536]{1,0:T(8,128)(2,1)} %get-tuple-element.7.link_in), custom_call_target="tpu_custom_call" | custom-call | tf_op jit(solution)/shard_map/pallas_call | solution.py:530

commit v7 on v5

--- a/solution.py
+++ b/solution.py
@@ -97,8 +97,8 @@
             for s in range(len(self.streams))[begin:end]:
                 self.at(s, 1).start()
 
-        def arrive(self, step):
-            for s, stream in enumerate(self.streams):
+        def arrive(self, step, begin=0, end=None):
+            for s, stream in list(enumerate(self.streams))[begin:end]:
                 if step <= stream[4]:
                     self.at(s, step).wait_recv()
                     if step < stream[4]:
@@ -348,14 +348,16 @@
 
     @pl.when(outer)
     def _():
+        ring_x.start(0, 2)
         times(link_scaled, y_all, take_left)
 
         @pl.when(role == 0)
         def _():
             even_result()
 
+        ring_x.arrive(1, 0, 2)
         pl.semaphore_wait(go, 1)
-        ring_x.start()
+        ring_x.start(2)
 
         def outer_cells(step):
             square_cell(step)
@@ -369,7 +371,7 @@
             for d in reach[step]:
                 put(final_cells, d, dot(far_left, x_rows(d)))
 
-        ring_x.arrive(1)
+        ring_x.arrive(1, 2)
         ring_x.arrive(2)
         hand_back.wait_recv()
 

time: 111 us -> 111 us (level)
  no operation moved by 1% of the time
where the time goes in v7:
time: 111 us
  Pallas kernels  110 us (99%)
    pallas_call x1, Pallas kernels, on_device(): pl.pallas_call(functools.partial(kernel, ring, parts), out_shape=(jax.Sha...  107 us
    pallas_call x1, Pallas kernels, on_device(): pl.pallas_call(finish, out_shape=(jax.ShapeDtypeStruct((rows, width), jnp...  2.59 us

profile of v7, /device:TPU:11, one launch (start us, length us, event | category | flops | bytes accessed | tf_op | source)
XLA Modules:
  0.0 110.6 jit_solution(17956614182532740719)
XLA Ops:
  0.6 107.3 %shard_map.59 = (bf16[192,1536]{1,0:T(8,128)(2,1)}, bf16[192,1536]{1,0:T(8,128)(2,1)}) custom-call(f32[192,1536]{1,0:T(8,128)} %bitcast.5, bf16[192,1536]{1,0:T(8,128)(2,1)} %bitcast.8, bf16[192,1536]{1,0:T(8,128)(2,1)} %bitcast.9, f32[1,1536]{1,0:T(1,128)} %diag_ref.1), custom_call_target="tpu_custom_call" | custom-call | flops 6341787648 | bytes 2949120 | tf_op jit(solution)/shard_map/pallas_call | solution.py:490
  108.0 2.6 %shard_map.60 = (f32[192,1536]{1,0:T(8,128)}, bf16[192,1536]{1,0:T(8,128)(2,1)}) custom-call(f32[192,1536]{1,0:T(8,128)} %bitcast.6, bf16[192,1536]{1,0:T(8,128)(2,1)} %get-tuple-element.6.taken_in, bf16[192,1536]{1,0:T(8,128)(2,1)} %get-tuple-element.7.link_in), custom_call_target="tpu_custom_call" | custom-call | tf_op jit(solution)/shard_map/pallas_call | solution.py:514
